TPU v7x, 1024 devices: a whole 4x4x32 slice. The times are simulated.
1024 devices in a mesh: dp: 16 (over y, x), mp: 64 (over z, core).
Axes of the slice: x: 4, y: 4, z: 32, core: 2. Of those that a mesh axis runs over, the one named last changes fastest.
Arguments:
- acts: bfloat16 [64, 8192, 512], P('mp', 'dp'), may hold values from -6 to 6
- outgrads: bfloat16 [64, 8192, 512], P('mp', 'dp'), may hold values from -6 to 6
- grad: bfloat16 [64, 512, 512], P(None, None, 'mp'), may hold values from -6 to 6
- owners: int32 [64, 2], P('mp'), may hold values from 0 to 15, all different within a row
Outputs:
- kept_roots: float32 [16, 64, 2, 512, 512], P('dp', 'mp')
- precond: float32 [64, 512, 512], P(None, None, 'mp')
Inputs may be any that keep to these rules, and one draw needn't show every extreme that they name: The two owners of a tile are different; every dp index owns some root.
All inputs are finite; a program needn't handle non-finite values.
Results may differ from a plain program's by a relative error of at most 0.006.
Values may be sent and summed in bfloat16 or wider, within the bound.
No kernel may reach another device: no remote copies, remote signals or barrier semaphores. Data moves between devices by JAX's collectives and lax.ppermute only.
A program may use at most 32 MiB of HBM per device.

v0:
```python
import jax
import jax.numpy as jnp
from jax import lax
from jax.sharding import PartitionSpec as P

ITERS = 2


damping = 0.001


def broadcast(value, axis, source):
    kept = jnp.where(lax.axis_index(axis) == source, value, 0).astype(value.dtype)
    return lax.psum(kept, axis)


def newton(stat):
    eye = jnp.eye(stat.shape[0], dtype=jnp.float32)
    scale = jnp.sqrt(jnp.sum(stat * stat))
    matrix = stat / scale
    root = eye * scale ** (-0.25)
    for turn in range(ITERS):
        factor = (5.0 * eye - matrix) * 0.25
        root = jnp.dot(root, factor, precision=lax.Precision.HIGHEST)
        if turn + 1 < ITERS:
            square = jnp.dot(factor, factor, precision=lax.Precision.HIGHEST)
            matrix = jnp.dot(
                square,
                jnp.dot(square, matrix, precision=lax.Precision.HIGHEST),
                precision=lax.Precision.HIGHEST,
            )
    return root


def vacant(stat):
    return jnp.zeros_like(stat)


def body(acts, outgrads, grad, owners):
    width = acts.shape[2]
    groups = lax.axis_size("dp")
    total_tokens = acts.shape[1] * groups
    eye = jnp.eye(width, dtype=jnp.float32)
    tile = lax.all_to_all(grad, "mp", split_axis=0, concat_axis=2, tiled=True)
    left_part = lax.dot_general(
        acts[0], acts[0], (((0,), (0,)), ((), ())), preferred_element_type=jnp.float32
    )
    right_part = lax.dot_general(
        outgrads[0], outgrads[0], (((0,), (0,)), ((), ())), preferred_element_type=jnp.float32
    )
    myself = lax.axis_index("dp")
    left_owner = owners[0, 0]
    right_owner = owners[0, 1]
    left_rows, right_rows = (
        lax.psum_scatter(left_part, "dp", scatter_dimension=0, tiled=True),
        lax.psum_scatter(right_part, "dp", scatter_dimension=0, tiled=True),
    )
    slots = jnp.arange(groups, dtype=jnp.int32)
    left_marks = (slots == left_owner).astype(jnp.float32)[:, None, None]
    right_marks = (slots == right_owner).astype(jnp.float32)[:, None, None]
    left_slots = left_marks * left_rows[None]
    right_slots = right_marks * right_rows[None]
    left_whole, right_whole = (
        lax.all_to_all(left_slots, "dp", split_axis=0, concat_axis=0, tiled=True),
        lax.all_to_all(right_slots, "dp", split_axis=0, concat_axis=0, tiled=True),
    )
    left_stat = left_whole.reshape(width, width) / total_tokens + damping * eye
    right_stat = right_whole.reshape(width, width) / total_tokens + damping * eye
    left_root = lax.cond(left_owner == myself, newton, vacant, left_stat)
    right_root = lax.cond(right_owner == myself, newton, vacant, right_stat)
    left_low = broadcast(left_root.astype(jnp.bfloat16), "dp", left_owner)
    right_low = broadcast(right_root.astype(jnp.bfloat16), "dp", right_owner)
    kept = jnp.stack([left_root, right_root])[None, None]
    half = jnp.dot(left_low, tile[0], preferred_element_type=jnp.float32).astype(jnp.bfloat16)
    mixed = jnp.dot(half, right_low, preferred_element_type=jnp.float32)
    precond = lax.all_to_all(mixed[None], "mp", split_axis=2, concat_axis=0, tiled=True)
    return (kept, precond)


def solution(mesh):
    in_specs = (P("mp", "dp", None), P("mp", "dp", None), P(None, None, "mp"), P("mp", None))
    out_specs = (P("dp", "mp", None, None, None), P(None, None, "mp"))
    return jax.shard_map(body, mesh=mesh, in_specs=in_specs, out_specs=out_specs, check_vma=False)
```

profile of v0, /device:TPU:1, one launch (start us, length us, event | category | flops | bytes accessed | tf_op | source)
XLA Modules:
  0.0 614.6 jit_solution(15091129337661576796)
XLA Ops:
  7.2 1.0 copy-done
  8.2 1.4 fusion.45
  9.7 1.4 fusion.47
  12.5 116.8 %reduce-scatter.5.cloned.1.call-done = f32[32,512]{1,0:T(8,128)} async-done(((f32[512,512]{1,0:T(8,128)}), f32[32,512]{1,0:T(8,128)}) %reduce-scatter.5.cloned.1.call-update) | async-done | bytes 65552 | tf_op jit(solution)/shard_map/reduce_scatter | solution.py:56
  129.3 1.9 broadcast_multiply_fusion
  131.2 4.5 all-to-all-start.1
  136.3 108.0 %reduce-scatter.3.cloned.1.call-done = f32[32,512]{1,0:T(8,128)} async-done(((f32[512,512]{1,0:T(8,128)}), f32[32,512]{1,0:T(8,128)}) %reduce-scatter.3.cloned.1.call-update) | async-done | bytes 65552 | tf_op jit(solution)/shard_map/reduce_scatter | solution.py:55
  244.3 1.0 broadcast_multiply_fusion.1
  245.3 18.5 %all_to_all.43 = f32[16,32,512]{2,1,0:T(8,128)} all-to-all(f32[16,32,512]{2,1,0:T(8,128)S(1)} %broadcast_multiply_fusion.1), channel_id=1, replica_groups=mesh['dp'=16,'mp'=64] {'dp'}, dimensions={0} | all-to-all | bytes 2097152 | tf_op jit(solution)/shard_map/all_to_all | solution.py:64
  263.8 27.3 %all-to-all-start.2 = ((bf16[64,512,8]{1,2,0:T(8,128)(2,1)}), bf16[64,512,8]{1,2,0:T(8,128)(2,1)}, u32[]{:S(2)}, u32[]{:S(2)}) async-start(bf16[64,512,8]{1,2,0:T(8,128)(2,1)} %param.10), calls=%async_computation.4 | async-start | bytes 1048576 | tf_op jit(solution)/shard_map/all_to_all | solution.py:44
  293.8 1.0 copy-done.4
  294.8 1.3 conditional.3
  294.8 1.1 stack.18
  296.1 2.0 conditional.2
  296.1 1.1 stack.16
  297.3 0.8 broadcast.56
  298.1 1.0 broadcast_select_fusion
  299.2 170.4 %all-reduce.3.cloned.1.call-done = (bf16[512,512]{1,0:T(8,128)(2,1)}, bf16[512,512]{1,0:T(8,128)(2,1)}) async-done(((bf16[512,512]{1,0:T(8,128)(2,1)}, bf16[512,512]{1,0:T(8,128)(2,1)}), (bf16[512,512]{1,0:T(8,128)(2,1)}, bf16[512,512]{1,0:T(8,128)(2,1)})) %all-reduce.3.cloned.1.call-update) | async-done | bytes 1048592 | tf_op jit(solution)/shard_map/psum | solution.py:14
  469.6 2.1 convolution_bitcast_fusion
  471.6 1.9 copy.8
  473.6 25.3 %all-to-all-start.3 = ((f32[1,512,512]{1,0,2:T(1,128)}), f32[1,512,512]{1,0,2:T(1,128)S(1)}, u32[]{:S(2)}, u32[]{:S(2)}) async-start(f32[1,512,512]{1,0,2:T(1,128)} %copy.8), calls=%async_computation.5 | async-start | bytes 2097152 | tf_op jit(solution)/shard_map/all_to_all | solution.py:76
  498.9 3.0 maximum_bitcast_fusion
  501.9 105.1 %all-to-all-done.3 = f32[1,512,512]{1,0,2:T(1,128)S(1)} async-done(((f32[1,512,512]{1,0,2:T(1,128)}), f32[1,512,512]{1,0,2:T(1,128)S(1)}, u32[]{:S(2)}, u32[]{:S(2)}) %all-to-all-start.3) | async-done | bytes 1048608 | tf_op jit(solution)/shard_map/all_to_all | solution.py:76
  607.1 1.0 copy.11
  (22 shorter events, 2.3 us)
Async XLA Ops:
  7.2 1.0 copy-start
  7.2 2.6 copy-start.6
  7.2 122.1 %reduce-scatter.5.cloned.1.call-start = ((), (), s32[]{:S(2)}) async-start(), calls=%async_computation.7 | async-start | bytes 1114112 | tf_op jit(solution)/shard_map/reduce_scatter | solution.py:56
  9.7 1.6 copy-start.7
  9.7 234.6 %reduce-scatter.3.cloned.1.call-start = ((), (), s32[]{:S(2)}) async-start(), calls=%async_computation.6 | async-start | bytes 1114112 | tf_op jit(solution)/shard_map/reduce_scatter | solution.py:55
  131.2 114.0 %all-to-all-start.1 = ((f32[16,32,512]{2,1,0:T(8,128)}), f32[16,32,512]{2,1,0:T(8,128)S(1)}, u32[]{:S(2)}, u32[]{:S(2)}) async-start(f32[16,32,512]{2,1,0:T(8,128)} %broadcast_multiply_fusion), calls=%async_computation.3 | async-start | bytes 2097152 | tf_op jit(solution)/shard_map/all_to_all | solution.py:65
  245.2 48.3 %copy-start.3 = (f32[16,32,512]{2,1,0:T(8,128)}, f32[16,32,512]{2,1,0:T(8,128)S(1)}, u32[]{:S(2)}) copy-start(f32[16,32,512]{2,1,0:T(8,128)S(1)} %all-to-all-done.1) | copy-start | bytes 3145732
  263.8 205.8 %all-to-all-start.2 = ((bf16[64,512,8]{1,2,0:T(8,128)(2,1)}), bf16[64,512,8]{1,2,0:T(8,128)(2,1)}, u32[]{:S(2)}, u32[]{:S(2)}) async-start(bf16[64,512,8]{1,2,0:T(8,128)(2,1)} %param.10), calls=%async_computation.4 | async-start | bytes 1048576 | tf_op jit(solution)/shard_map/all_to_all | solution.py:44
  291.1 178.5 %all-reduce.3.cloned.1.call-start = ((), (), s32[]{:S(2)}) async-start(), calls=%async_computation.8 | async-start | bytes 2097152 | tf_op jit(solution)/shard_map/psum | solution.py:14
  293.6 1.2 copy-start.4
  473.6 133.5 %all-to-all-start.3 = ((f32[1,512,512]{1,0,2:T(1,128)}), f32[1,512,512]{1,0,2:T(1,128)S(1)}, u32[]{:S(2)}, u32[]{:S(2)}) async-start(f32[1,512,512]{1,0,2:T(1,128)} %copy.8), calls=%async_computation.5 | async-start | bytes 2097152 | tf_op jit(solution)/shard_map/all_to_all | solution.py:76
Sparse Core Ops, SparseCore 0:
  13.8 115.3 reduce-scatter.4
  135.9 108.3 reduce-scatter.2
  299.3 170.2 all-reduce.2
where the time goes:
time: 616 us; the launch traced here: 615 us
  waiting for transfers between devices  500 us (81%)
  starting transfers between devices  57.2 us (9%)
  blocking collectives  18.5 us (3%)
  between operations  16.3 us (3%)
  local copies, waits for them, and re-layouts  8.78 us (1%)
  other arithmetic  8.31 us (1%)
    psum x1, waiting for transfers between devices, broadcast(): return lax.psum(kept, axis)  170 us
    reduce_scatter x1, waiting for transfers between devices, body(): lax.psum_scatter(right_part, 'dp', scatter_dimension=0, tiled=True)  117 us
    reduce_scatter x1, waiting for transfers between devices, body(): lax.psum_scatter(left_part, 'dp', scatter_dimension=0, tiled=True)  108 us
    all_to_all x1, waiting for transfers between devices, body(): lax.all_to_all(mixed[None], 'mp', split_axis=2, concat_axis=0, tiled=True)  105 us
    all_to_all x1, starting transfers between devices, body(): tile = lax.all_to_all(grad, 'mp', split_axis=0, concat_axis=2, tiled=True)  27.3 us
    all_to_all x1, starting transfers between devices, body(): lax.all_to_all(mixed[None], 'mp', split_axis=2, concat_axis=0, tiled=True)  25.3 us
    all_to_all x1, blocking collectives, body(): lax.all_to_all(left_slots, 'dp', split_axis=0, concat_axis=0, tiled=True)  18.5 us
  transfers between devices with their start and end apart: 6, of which 4 were waited for; matrix products, arithmetic and copies ran while one was open for 2% of the time, Pallas kernels for 0%

commit v1 on v0

v1 whole, which is shorter than its diff:
```python
import functools

import jax
import jax.numpy as jnp
from jax import lax
from jax.experimental import pallas as pl
from jax.experimental.pallas import tpu as pltpu
from jax.sharding import Mesh, PartitionSpec as P

damping = 0.001
SIDE = 128
LIMIT = 48 * 1024 * 1024


def blocks(width):
    n = width // SIDE
    return [(i, j) for i in range(n) for j in range(i, n)]


def gram_kernel(acts_ref, outs_ref, packed_ref, held_ref, sems):
    tokens, width = acts_ref.shape[1:]
    places = blocks(width)
    wide = 2 * SIDE
    copies = []
    for which, ref in enumerate((acts_ref, outs_ref)):
        for part in range(2):
            span = pl.ds(part * (tokens // 2), tokens // 2)
            copies.append(pltpu.make_async_copy(ref.at[0, span], held_ref.at[which, span], sems.at[which, part]))
            copies[-1].start()
    for which in range(2):
        base = which * len(places)
        copies[2 * which].wait()
        copies[2 * which + 1].wait()
        for i in range(0, width, wide):
            left = held_ref[which, :, i : i + wide]
            part = lax.dot_general(
                left, held_ref[which, :, i:], (((0,), (0,)), ((), ())), preferred_element_type=jnp.float32
            )
            for spot, (r, c) in enumerate(places):
                if i <= r * SIDE < i + wide:
                    row, col = r * SIDE - i, c * SIDE - i
                    packed_ref[pl.ds((base + spot) * SIDE, SIDE), :] = part[
                        row : row + SIDE, col : col + SIDE
                    ].astype(packed_ref.dtype)


def sum_kernel(total_tokens, parts_ref, shards_ref, copies_ref):
    count, rows = parts_ref.shape[:2]
    tall, width = shards_ref.shape[1:]
    for tile in range(2):
        total = parts_ref[tile].astype(jnp.float32)
        for g in range(2 + tile, count, 2):
            total = total + parts_ref[g].astype(jnp.float32)
        total = (total / total_tokens).astype(copies_ref.dtype)
        for g in range(tile, count, 2):
            copies_ref[g, :rows] = total
            for lane in range(width // SIDE):
                copies_ref[g, pl.ds(rows + lane * tall, tall)] = shards_ref[tile, :, lane * SIDE : (lane + 1) * SIDE]


def mm(a, b):
    return jnp.dot(a.astype(jnp.bfloat16), b.astype(jnp.bfloat16), preferred_element_type=jnp.float32)


def diag(width):
    rows = lax.broadcasted_iota(jnp.int32, (width, width), 0)
    cols = lax.broadcasted_iota(jnp.int32, (width, width), 1)
    return rows == cols


def root_kernel(coord_ref, mixed_ref, left_ref, right_ref, piece_ref, stat_ref, tile_ref):
    width = stat_ref.shape[0]
    places = blocks(width)
    on_diag = diag(width)
    for which, root_ref in enumerate((left_ref, right_ref)):
        base = which * len(places)
        share = 2 * len(places) * SIDE // mixed_ref.shape[0]
        for spot, (r, c) in enumerate(places):
            start, stop, pieces = (base + spot) * SIDE, (base + spot + 1) * SIDE, []
            while start < stop:
                size = min(stop, (start // share + 1) * share) - start
                pieces.append(mixed_ref[start // share, pl.ds(start % share, size)])
                start += size
            block = jnp.concatenate(pieces, axis=0).astype(jnp.float32)
            stat_ref[pl.ds(r * SIDE, SIDE), pl.ds(c * SIDE, SIDE)] = block
            if r != c:
                stat_ref[pl.ds(c * SIDE, SIDE), pl.ds(r * SIDE, SIDE)] = block.T
        stat = stat_ref[...] + jnp.where(on_diag, damping, 0.0)
        squares = jnp.sum(jnp.sum(stat * stat, axis=0, keepdims=True), axis=1, keepdims=True)
        inv_scale = 1.0 / jnp.sqrt(squares)
        matrix = stat * inv_scale
        low = matrix.astype(jnp.bfloat16)
        square = mm(low, low)
        shift = square * 0.0625 - matrix * 0.625
        shift_low = shift.astype(jnp.bfloat16)
        quart = mm(shift_low, shift_low) + 3.125 * shift + jnp.where(on_diag, 625.0 / 256.0, 0.0)
        lead = matrix * 1.25 - square * 0.25
        tail = mm(lead, quart)
        factor = jnp.sqrt(jnp.sqrt(inv_scale))
        root_ref[...] = factor * (jnp.where(on_diag, 1.5625, 0.0) - 0.3125 * matrix - 0.25 * tail)

    me, plane = coord_ref[0], coord_ref[1]
    count, planes, tall = mixed_ref.shape[0], mixed_ref.shape[0], 16
    side = tall // 2
    for d in range(count // 2):
        for lane in range(width // SIDE):
            low_rows = pl.ds(share + lane * tall, tall)
            even, odd = mixed_ref[2 * d, low_rows].astype(jnp.float32), mixed_ref[2 * d + 1, low_rows].astype(jnp.float32)
            for j in range(2):
                source = lax.rem(plane - shift_of(d, j) + 2 * planes, planes)
                both = jnp.concatenate([even[j * side : (j + 1) * side], odd[j * side : (j + 1) * side]])
                tile_ref[pl.ds(pl.multiple_of(source * tall, tall), tall), pl.ds(lane * SIDE, SIDE)] = both.astype(
                    tile_ref.dtype
                )
    half = mm(tile_ref[...], left_ref[...]).astype(jnp.bfloat16)
    strips = []
    for j in range(2):
        goal = lax.rem(plane + shift_of(me, j) + 2 * planes, planes)
        strips.append(right_ref[pl.ds(pl.multiple_of(goal * tall, tall), tall), :])
    product = mm(jnp.concatenate(strips, axis=0), half).astype(piece_ref.dtype)
    for j in range(2):
        piece_ref[j] = product[j * tall : (j + 1) * tall]


def place_kernel(coord_ref, every_ref, out_ref):
    plane, first = coord_ref[1], pl.program_id(0) * (out_ref.shape[0] // 2)
    planes = every_ref.shape[0]
    groups, half = planes // 2, every_ref.shape[1] // 2
    for p in range(out_ref.shape[0] // 2):
        turn = lax.rem(plane - first - p + groups // 2 + 2 * planes, planes)
        d, far = lax.rem(turn, groups), turn >= groups
        for core in range(2):
            block = every_ref[2 * d + core].astype(jnp.float32)
            out_ref[2 * p + core] = jnp.where(far, block[half:], block[:half])


def shift_of(d, j):
    return d - 8 if j == 0 else d + 8


def spread(near, far, groups):
    landed = jnp.concatenate([near, far], axis=1)
    landed = jnp.broadcast_to(landed[None], (groups,) + landed.shape)
    landed = landed.reshape((-1,) + landed.shape[2:])
    return lax.all_to_all(landed, ("dp", "core"), split_axis=0, concat_axis=0, tiled=True)


def carry(value, tiles, groups, planes, shift):
    pairs = [
        (d * tiles + 2 * p + c, d * tiles + 2 * ((p + shift(d)) % planes) + c)
        for d in range(groups)
        for p in range(planes)
        for c in range(2)
    ]
    return lax.ppermute(value, ("dp", "z", "core"), pairs)


def body(acts, outgrads, grad, owners):
    width = acts.shape[2]
    groups = lax.axis_size("dp")
    planes = lax.axis_size("z")
    tiles = 2 * planes
    total_tokens = acts.shape[1] * groups
    me, plane, core = lax.axis_index("dp"), lax.axis_index("z"), lax.axis_index("core")
    coords = jnp.stack([me, plane])
    vmem = pl.BlockSpec(memory_space=pltpu.VMEM)
    smem = pl.BlockSpec(memory_space=pltpu.SMEM)
    params = pltpu.CompilerParams(vmem_limit_bytes=LIMIT)
    rows = 2 * len(blocks(width)) * SIDE

    turned = jnp.transpose(grad, (0, 2, 1))
    shards = turned.shape[1]
    near, far = (
        lax.dynamic_slice(
            turned, (2 * lax.rem(plane + shift_of(me, j) + 2 * planes, planes), 0, 0), (2, shards, width)
        )
        for j in range(2)
    )
    packed = pl.pallas_call(
        gram_kernel,
        out_shape=jax.ShapeDtypeStruct((rows, SIDE), jnp.bfloat16),
        in_specs=[pl.BlockSpec(memory_space=pl.ANY)] * 2,
        out_specs=vmem,
        scratch_shapes=[pltpu.VMEM((2,) + acts.shape[1:], acts.dtype), pltpu.SemaphoreType.DMA((2, 2))],
        compiler_params=pltpu.CompilerParams(vmem_limit_bytes=60 * 1024 * 1024),
        name="gram",
    )(acts, outgrads)
    parts = lax.all_to_all(
        packed.reshape(2 * groups, rows // groups // 2, SIDE), ("dp", "core"), split_axis=0, concat_axis=0, tiled=True
    )
    near, far = (
        carry(sent, tiles, groups, planes, functools.partial(shift_of, j=j)) for j, sent in enumerate((near, far))
    )
    landed = jnp.concatenate([near, far], axis=1)
    copies = pl.pallas_call(
        functools.partial(sum_kernel, total_tokens),
        out_shape=jax.ShapeDtypeStruct(
            (2 * groups, rows // groups // 2 + 2 * shards * width // SIDE, SIDE), jnp.bfloat16
        ),
        in_specs=[vmem, vmem],
        out_specs=vmem,
        compiler_params=params,
        name="sum",
    )(parts, landed)
    mixed = lax.all_to_all(copies, ("dp", "core"), split_axis=0, concat_axis=0, tiled=True)
    left_root, right_root, piece = pl.pallas_call(
        root_kernel,
        out_shape=(
            jax.ShapeDtypeStruct((width, width), jnp.float32),
            jax.ShapeDtypeStruct((width, width), jnp.float32),
            jax.ShapeDtypeStruct((2, 2 * shards, width), jnp.bfloat16),
        ),
        in_specs=[smem, vmem],
        out_specs=(vmem, vmem, vmem),
        scratch_shapes=[pltpu.VMEM((width, width), jnp.float32), pltpu.VMEM((width, width), jnp.bfloat16)],
        compiler_params=params,
        name="roots",
    )(coords, mixed)
    kept = jnp.stack(
        [jnp.where(owners[0, which] == me, root, 0.0) for which, root in enumerate((left_root, right_root))]
    )[None, None]

    landed = [
        carry(piece[j].reshape(2, shards, width), tiles, groups, planes, functools.partial(shift_of, j=j))
        for j in range(2)
    ]
    every = spread(*landed, groups)
    placed = pl.pallas_call(
        place_kernel,
        out_shape=jax.ShapeDtypeStruct((tiles, shards, width), jnp.float32),
        grid=(4,),
        in_specs=[smem, vmem],
        out_specs=pl.BlockSpec((tiles // 4, shards, width), lambda part: (part, 0, 0)),
        compiler_params=params,
        name="place",
    )(coords, every)
    return (kept, jnp.transpose(placed, (0, 2, 1)))


def solution(mesh):
    split = Mesh(mesh.devices.reshape(mesh.shape["dp"], -1, 2), ("dp", "z", "core"))
    mp = ("z", "core")
    in_specs = (P(mp, "dp", None), P(mp, "dp", None), P(None, None, mp), P(mp, None))
    out_specs = (P("dp", mp, None, None, None), P(None, None, mp))
    return jax.shard_map(body, mesh=split, in_specs=in_specs, out_specs=out_specs, check_vma=False)
```

time: 616 us -> 128 us (0.21)
  waiting for transfers between devices: 500 us -> 45.6 us
  blocking collectives: 18.5 us -> 0 us
  between operations: 16.3 us -> 2.05 us
  Pallas kernels: 0 us -> 9.78 us
  starting transfers between devices: 57.2 us -> 66.1 us
  local copies, waits for them, and re-layouts: 8.78 us -> 2.21 us
  other arithmetic: 8.31 us -> 1.8 us
    reduce_scatter x2 -> x0, waiting for transfers between devices: 225 us -> none  [the longest x1 117 us: body(): lax.psum_scatter(right_part, 'dp', scatter_dimension=0, tiled=True)]
    psum x1 -> x0, waiting for transfers between devices: 170 us -> none  [broadcast(): return lax.psum(kept, axis)]
    all_to_all x3, waiting for transfers between devices: 105 us -> 25.5 us  [the longest x1 17.6 us: body(): lax.all_to_all(copies, ('dp', 'core'), split_axis=0, concat_axis=0, tiled...]
    ppermute x0 -> x4, starting transfers between devices: none -> 29.5 us  [carry(): return lax.ppermute(value, ('dp', 'z', 'core'), pairs)]
    all_to_all x3, starting transfers between devices: 57.1 us -> 36.6 us  [the longest x1 17.7 us: body(): lax.all_to_all(packed.reshape(2 * groups, rows // groups // 2, SIDE), ('d...]
    ppermute x0 -> x4, waiting for transfers between devices: none -> 20.1 us  [carry(): return lax.ppermute(value, ('dp', 'z', 'core'), pairs)]
    all_to_all x1 -> x0, blocking collectives: 18.5 us -> none  [body(): lax.all_to_all(left_slots, 'dp', split_axis=0, concat_axis=0, tiled=True)]
    pallas_call x0 -> x4, Pallas kernels: none -> 9.78 us  [the longest x1 3.66 us: body(): pl.pallas_call(root_kernel, out_shape=(jax.ShapeDtypeStruct((width, width...]
  transfers between devices with their start and end apart: 6 -> 7, of which waited for: 4 -> 4; matrix products, arithmetic and copies ran while one was open for 2% -> 2% of each run, Pallas kernels for 0% -> 0%
where the time goes in v1:
time: 128 us
  starting transfers between devices  66.1 us (52%)
  waiting for transfers between devices  45.6 us (36%)
  Pallas kernels  9.78 us (8%)
  local copies, waits for them, and re-layouts  2.21 us (2%)
  between operations  2.05 us (2%)
  other arithmetic  1.8 us (1%)
    ppermute x4, starting transfers between devices, carry(): return lax.ppermute(value, ('dp', 'z', 'core'), pairs)  29.5 us
    ppermute x4, waiting for transfers between devices, carry(): return lax.ppermute(value, ('dp', 'z', 'core'), pairs)  20.1 us
    all_to_all x1, starting transfers between devices, body(): lax.all_to_all(packed.reshape(2 * groups, rows // groups // 2, SIDE), ('d...  17.7 us
    all_to_all x1, waiting for transfers between devices, body(): lax.all_to_all(copies, ('dp', 'core'), split_axis=0, concat_axis=0, tiled...  17.6 us
    all_to_all x1, starting transfers between devices, body(): lax.all_to_all(copies, ('dp', 'core'), split_axis=0, concat_axis=0, tiled...  11.5 us
    all_to_all x1, waiting for transfers between devices, spread(): lax.all_to_all(landed, ('dp', 'core'), split_axis=0, concat_axis=0, tiled...  7.92 us
    all_to_all x1, starting transfers between devices, spread(): lax.all_to_all(landed, ('dp', 'core'), split_axis=0, concat_axis=0, tiled...  7.36 us
    pallas_call x1, Pallas kernels, body(): pl.pallas_call(root_kernel, out_shape=(jax.ShapeDtypeStruct((width, width...  3.66 us
  transfers between devices with their start and end apart: 7, of which 4 were waited for; matrix products, arithmetic and copies ran while one was open for 2% of the time, Pallas kernels for 0%

profile of v1, /device:TPU:1, one launch (start us, length us, event | category | flops | bytes accessed | tf_op | source)
XLA Modules:
  0.0 127.6 jit_solution(11002299274096911509)
XLA Ops:
  0.6 2.8 %gram.1 = bf16[2560,128]{1,0:T(8,128)(2,1)} custom-call(bf16[1,512,512]{2,1,0:T(8,128)(2,1)} %acts_ref.1, bf16[1,512,512]{2,1,0:T(8,128)(2,1)} %outs_ref.1), custom_call_target="tpu_custom_call" | custom-call | tf_op jit(solution)/shard_map/gram/pallas_call | solution.py:179
  3.5 17.7 %all-to-all-start = ((bf16[32,80,128]{2,1,0:T(8,128)(2,1)}), bf16[32,80,128]{2,1,0:T(8,128)(2,1)S(1)}, u32[]{:S(2)}, u32[]{:S(2)}) async-start(bf16[32,80,128]{2,1,0:T(8,128)(2,1)} %bitcast.21), calls=%async_computation | async-start | bytes 1310720 | tf_op jit(solution)/shard_map/all_to_all | solution.py:188
  21.2 0.7 dynamic-slice_bitcast_fusion.1
  22.0 13.6 %collective-permute-start = (bf16[2,8,512]{2,1,0:T(8,128)(2,1)S(1)}, bf16[2,8,512]{2,1,0:T(8,128)(2,1)S(1)}, u32[]{:S(2)}, u32[]{:S(2)}) collective-permute-start(bf16[2,8,512]{2,1,0:T(8,128)(2,1)S(1)} %get-tuple-element.8), channel_id=1, source_target_pairs={{0,48},{1,49},{2,50},{3,51},{4,52},{5,53},{6,54},{7,55},{8,56},{9,... | collective-permute-start | bytes 49160 | tf_op jit(solution)/shard_map/ppermute | solution.py:155
  35.5 1.9 %collective-permute-start.1 = (bf16[2,8,512]{2,1,0:T(8,128)(2,1)S(1)}, bf16[2,8,512]{2,1,0:T(8,128)(2,1)S(1)}, u32[]{:S(2)}, u32[]{:S(2)}) collective-permute-start(bf16[2,8,512]{2,1,0:T(8,128)(2,1)S(1)} %get-tuple-element.9), channel_id=1, source_target_pairs={{0,16},{1,17},{2,18},{3,19},{4,20},{5,21},{6,22},{7,23},{8,24},{9,... | collective-permute-start | bytes 49160 | tf_op jit(solution)/shard_map/ppermute | solution.py:155
  37.5 0.0 collective-permute-done
  37.5 11.3 %collective-permute-done.1 = bf16[2,8,512]{2,1,0:T(8,128)(2,1)S(1)} collective-permute-done((bf16[2,8,512]{2,1,0:T(8,128)(2,1)S(1)}, bf16[2,8,512]{2,1,0:T(8,128)(2,1)S(1)}, u32[]{:S(2)}, u32[]{:S(2)}) %collective-permute-start.1) | collective-permute-done | bytes 16416 | tf_op jit(solution)/shard_map/ppermute | solution.py:155
  48.8 0.0 all-to-all-done.parts_ref
  48.8 1.2 sum.1
  49.9 11.5 %all-to-all-start.1 = ((bf16[32,144,128]{2,1,0:T(8,128)(2,1)}), bf16[32,144,128]{2,1,0:T(8,128)(2,1)S(1)}, u32[]{:S(2)}, u32[]{:S(2)}) async-start(bf16[32,144,128]{2,1,0:T(8,128)(2,1)} %sum.1), calls=%async_computation.1 | async-start | bytes 2359296 | tf_op jit(solution)/shard_map/all_to_all | solution.py:205
  61.4 0.1 pad_add_fusion.coord_ref
  61.5 17.6 %all-to-all-done.1.mixed_ref = bf16[32,144,128]{2,1,0:T(8,128)(2,1)S(1)} async-done(((bf16[32,144,128]{2,1,0:T(8,128)(2,1)}), bf16[32,144,128]{2,1,0:T(8,128)(2,1)S(1)}, u32[]{:S(2)}, u32[]{:S(2)}) %all-to-all-start.1) | async-done | bytes 1179680 | tf_op jit(solution)/shard_map/all_to_all | solution.py:205
  79.1 3.7 %roots.1 = (f32[512,512]{1,0:T(8,128)S(1)}, f32[512,512]{1,0:T(8,128)S(1)}, bf16[2,16,512]{2,1,0:T(8,128)(2,1)S(1)}) custom-call(s32[2]{0:T(128)S(1)} %pad_add_fusion.coord_ref, bf16[32,144,128]{2,1,0:T(8,128)(2,1)S(1)} %all-to-all-done.1.mixed_ref), custom_call_target="tpu_custom_call" | custom-call | tf_op jit(solution)/shard_map/roots/pallas_call | solution.py:206
  82.8 9.7 %collective-permute-start.2 = (bf16[2,8,512]{2,1,0:T(8,128)(2,1)S(1)}, bf16[2,8,512]{2,1,0:T(8,128)(2,1)S(1)}, u32[]{:S(2)}, u32[]{:S(2)}) collective-permute-start(bf16[2,8,512]{2,1,0:T(8,128)(2,1)S(1)} %get-tuple-element.10), channel_id=1, source_target_pairs={{0,48},{1,49},{2,50},{3,51},{4,52},{5,53},{6,54},{7,55},{8,56},{9,... | collective-permute-start | bytes 49160 | tf_op jit(solution)/shard_map/ppermute | solution.py:155
  92.5 4.3 %collective-permute-start.3 = (bf16[2,8,512]{2,1,0:T(8,128)(2,1)S(1)}, bf16[2,8,512]{2,1,0:T(8,128)(2,1)S(1)}, u32[]{:S(2)}, u32[]{:S(2)}) collective-permute-start(bf16[2,8,512]{2,1,0:T(8,128)(2,1)S(1)} %get-tuple-element.11), channel_id=1, source_target_pairs={{0,16},{1,17},{2,18},{3,19},{4,20},{5,21},{6,22},{7,23},{8,24},{9,... | collective-permute-start | bytes 49160 | tf_op jit(solution)/shard_map/ppermute | solution.py:155
  96.8 0.0 collective-permute-done.2
  96.8 8.8 %collective-permute-done.3 = bf16[2,8,512]{2,1,0:T(8,128)(2,1)S(1)} collective-permute-done((bf16[2,8,512]{2,1,0:T(8,128)(2,1)S(1)}, bf16[2,8,512]{2,1,0:T(8,128)(2,1)S(1)}, u32[]{:S(2)}, u32[]{:S(2)}) %collective-permute-start.3) | collective-permute-done | bytes 16416 | tf_op jit(solution)/shard_map/ppermute | solution.py:155
  105.7 0.9 broadcast_in_dim.16
  106.5 7.4 %all-to-all-start.2 = ((bf16[32,16,512]{2,1,0:T(8,128)(2,1)}), bf16[32,16,512]{2,1,0:T(8,128)(2,1)S(1)}, u32[]{:S(2)}, u32[]{:S(2)}) async-start(bf16[32,16,512]{2,1,0:T(8,128)(2,1)} %bitcast.12), calls=%async_computation.2 | async-start | bytes 1048576 | tf_op jit(solution)/shard_map/all_to_all | solution.py:145
  113.9 0.6 fusion
  115.8 0.2 select_bitcast_fusion
  116.0 1.5 %maximum_bitcast_fusion = f32[1,1,2,512,512]{4,3,2,1,0:T(8,128)} fusion(f32[1,512,512]{2,1,0:T(8,128)S(1)} %get-tuple-element.14, f32[1,512,512]{2,1,0:T(8,128)S(1)} %get-tuple-element.15), kind=kLoop, calls=%fused_computation | loop fusion | flops 524288 | bytes 4194304 | tf_op jit(solution)/shard_map/broadcast_in_dim | solution.py:219
  117.5 7.9 %all-to-all-done.2.every_ref = bf16[32,16,512]{2,1,0:T(8,128)(2,1)S(1)} async-done(((bf16[32,16,512]{2,1,0:T(8,128)(2,1)}), bf16[32,16,512]{2,1,0:T(8,128)(2,1)S(1)}, u32[]{:S(2)}, u32[]{:S(2)}) %all-to-all-start.2) | async-done | bytes 524320 | tf_op jit(solution)/shard_map/all_to_all | solution.py:145
  125.5 2.1 %place.1 = f32[64,8,512]{2,1,0:T(8,128)} custom-call(s32[2]{0:T(128)S(1)} %pad_add_fusion.coord_ref, bf16[32,16,512]{2,1,0:T(8,128)(2,1)S(1)} %all-to-all-done.2.every_ref), custom_call_target="tpu_custom_call" | custom-call | tf_op jit(solution)/shard_map/place/pallas_call | solution.py:228
  (5 shorter events, 0.0 us)
Async XLA Ops:
  3.5 45.3 %all-to-all-start = ((bf16[32,80,128]{2,1,0:T(8,128)(2,1)}), bf16[32,80,128]{2,1,0:T(8,128)(2,1)S(1)}, u32[]{:S(2)}, u32[]{:S(2)}) async-start(bf16[32,80,128]{2,1,0:T(8,128)(2,1)} %bitcast.21), calls=%async_computation | async-start | bytes 1310720 | tf_op jit(solution)/shard_map/all_to_all | solution.py:188
  22.0 15.5 %collective-permute-start = (bf16[2,8,512]{2,1,0:T(8,128)(2,1)S(1)}, bf16[2,8,512]{2,1,0:T(8,128)(2,1)S(1)}, u32[]{:S(2)}, u32[]{:S(2)}) collective-permute-start(bf16[2,8,512]{2,1,0:T(8,128)(2,1)S(1)} %get-tuple-element.8), channel_id=1, source_target_pairs={{0,48},{1,49},{2,50},{3,51},{4,52},{5,53},{6,54},{7,55},{8,56},{9,... | collective-permute-start | bytes 49160 | tf_op jit(solution)/shard_map/ppermute | solution.py:155
  35.5 13.2 %collective-permute-start.1 = (bf16[2,8,512]{2,1,0:T(8,128)(2,1)S(1)}, bf16[2,8,512]{2,1,0:T(8,128)(2,1)S(1)}, u32[]{:S(2)}, u32[]{:S(2)}) collective-permute-start(bf16[2,8,512]{2,1,0:T(8,128)(2,1)S(1)} %get-tuple-element.9), channel_id=1, source_target_pairs={{0,16},{1,17},{2,18},{3,19},{4,20},{5,21},{6,22},{7,23},{8,24},{9,... | collective-permute-start | bytes 49160 | tf_op jit(solution)/shard_map/ppermute | solution.py:155
  49.9 64.0 %copy-start = (s32[1,2]{1,0:T(1,128)S(1)}, s32[1,2]{1,0:T(1,128)}, u32[]{:S(2)}) copy-start(s32[1,2]{1,0:T(1,128)} %param.7) | copy-start | bytes 28
  49.9 29.2 %all-to-all-start.1 = ((bf16[32,144,128]{2,1,0:T(8,128)(2,1)}), bf16[32,144,128]{2,1,0:T(8,128)(2,1)S(1)}, u32[]{:S(2)}, u32[]{:S(2)}) async-start(bf16[32,144,128]{2,1,0:T(8,128)(2,1)} %sum.1), calls=%async_computation.1 | async-start | bytes 2359296 | tf_op jit(solution)/shard_map/all_to_all | solution.py:205
  82.8 14.0 %collective-permute-start.2 = (bf16[2,8,512]{2,1,0:T(8,128)(2,1)S(1)}, bf16[2,8,512]{2,1,0:T(8,128)(2,1)S(1)}, u32[]{:S(2)}, u32[]{:S(2)}) collective-permute-start(bf16[2,8,512]{2,1,0:T(8,128)(2,1)S(1)} %get-tuple-element.10), channel_id=1, source_target_pairs={{0,48},{1,49},{2,50},{3,51},{4,52},{5,53},{6,54},{7,55},{8,56},{9,... | collective-permute-start | bytes 49160 | tf_op jit(solution)/shard_map/ppermute | solution.py:155
  92.5 13.2 %collective-permute-start.3 = (bf16[2,8,512]{2,1,0:T(8,128)(2,1)S(1)}, bf16[2,8,512]{2,1,0:T(8,128)(2,1)S(1)}, u32[]{:S(2)}, u32[]{:S(2)}) collective-permute-start(bf16[2,8,512]{2,1,0:T(8,128)(2,1)S(1)} %get-tuple-element.11), channel_id=1, source_target_pairs={{0,16},{1,17},{2,18},{3,19},{4,20},{5,21},{6,22},{7,23},{8,24},{9,... | collective-permute-start | bytes 49160 | tf_op jit(solution)/shard_map/ppermute | solution.py:155
  106.5 18.9 %all-to-all-start.2 = ((bf16[32,16,512]{2,1,0:T(8,128)(2,1)}), bf16[32,16,512]{2,1,0:T(8,128)(2,1)S(1)}, u32[]{:S(2)}, u32[]{:S(2)}) async-start(bf16[32,16,512]{2,1,0:T(8,128)(2,1)} %bitcast.12), calls=%async_computation.2 | async-start | bytes 1048576 | tf_op jit(solution)/shard_map/all_to_all | solution.py:145

commit v2 on v1

--- a/solution.py
+++ b/solution.py
@@ -99,23 +99,22 @@
         factor = jnp.sqrt(jnp.sqrt(inv_scale))
         root_ref[...] = factor * (jnp.where(on_diag, 1.5625, 0.0) - 0.3125 * matrix - 0.25 * tail)
 
-    me, plane = coord_ref[0], coord_ref[1]
-    count, planes, tall = mixed_ref.shape[0], mixed_ref.shape[0], 16
+    me, plane, my_core = coord_ref[0], coord_ref[1], coord_ref[2]
+    planes, tall = mixed_ref.shape[0], 16
     side = tall // 2
-    for d in range(count // 2):
+    for shift in range(planes):
+        source = pl.multiple_of(lax.rem(plane - shift + planes, planes) * tall, tall)
         for lane in range(width // SIDE):
-            low_rows = pl.ds(share + lane * tall, tall)
-            even, odd = mixed_ref[2 * d, low_rows].astype(jnp.float32), mixed_ref[2 * d + 1, low_rows].astype(jnp.float32)
-            for j in range(2):
-                source = lax.rem(plane - shift_of(d, j) + 2 * planes, planes)
-                both = jnp.concatenate([even[j * side : (j + 1) * side], odd[j * side : (j + 1) * side]])
-                tile_ref[pl.ds(pl.multiple_of(source * tall, tall), tall), pl.ds(lane * SIDE, SIDE)] = both.astype(
-                    tile_ref.dtype
-                )
+            both = []
+            for core in range(2):
+                d, j = holder_of(shift, core)
+                rows = mixed_ref[2 * d + core, pl.ds(share + lane * tall, tall)].astype(jnp.float32)
+                both.append(rows[j * side : (j + 1) * side])
+            tile_ref[pl.ds(source, tall), pl.ds(lane * SIDE, SIDE)] = jnp.concatenate(both).astype(tile_ref.dtype)
     half = mm(tile_ref[...], left_ref[...]).astype(jnp.bfloat16)
     strips = []
     for j in range(2):
-        goal = lax.rem(plane + shift_of(me, j) + 2 * planes, planes)
+        goal = lax.rem(plane + shift_of(me, my_core, j) + 2 * planes, planes)
         strips.append(right_ref[pl.ds(pl.multiple_of(goal * tall, tall), tall), :])
     product = mm(jnp.concatenate(strips, axis=0), half).astype(piece_ref.dtype)
     for j in range(2):
@@ -123,23 +122,28 @@
 
 
 def place_kernel(coord_ref, every_ref, out_ref):
-    plane, first = coord_ref[1], pl.program_id(0) * (out_ref.shape[0] // 2)
+    plane = coord_ref[1]
     planes = every_ref.shape[0]
-    groups, half = planes // 2, every_ref.shape[1] // 2
-    for p in range(out_ref.shape[0] // 2):
-        turn = lax.rem(plane - first - p + groups // 2 + 2 * planes, planes)
-        d, far = lax.rem(turn, groups), turn >= groups
-        for core in range(2):
-            block = every_ref[2 * d + core].astype(jnp.float32)
-            out_ref[2 * p + core] = jnp.where(far, block[half:], block[:half])
-
-
-def shift_of(d, j):
-    return d - 8 if j == 0 else d + 8
-
-
-def spread(near, far, groups):
-    landed = jnp.concatenate([near, far], axis=1)
+    half = every_ref.shape[1] // 2
+    for i in range(planes):
+        block = every_ref[i].astype(jnp.float32)
+        for j in range(2):
+            source = lax.rem(plane - shift_of(i // 2, i % 2, j) + 2 * planes, planes)
+            out_ref[2 * source + i % 2] = block[j * half : (j + 1) * half]
+
+
+def shift_of(d, core, j):
+    ahead = d + 8 if j == 0 else d - 8
+    return ahead * (1 - 2 * core)
+
+
+def holder_of(shift, core):
+    turn = ((1 - 2 * core) * shift + 8) % 32
+    return turn % 16, 1 - turn // 16
+
+
+def spread(far, near, groups):
+    landed = jnp.concatenate([far, near], axis=1)
     landed = jnp.broadcast_to(landed[None], (groups,) + landed.shape)
     landed = landed.reshape((-1,) + landed.shape[2:])
     return lax.all_to_all(landed, ("dp", "core"), split_axis=0, concat_axis=0, tiled=True)
@@ -147,7 +151,7 @@
 
 def carry(value, tiles, groups, planes, shift):
     pairs = [
-        (d * tiles + 2 * p + c, d * tiles + 2 * ((p + shift(d)) % planes) + c)
+        (d * tiles + 2 * p + c, d * tiles + 2 * ((p + shift(d, c)) % planes) + c)
         for d in range(groups)
         for p in range(planes)
         for c in range(2)
@@ -162,7 +166,7 @@
     tiles = 2 * planes
     total_tokens = acts.shape[1] * groups
     me, plane, core = lax.axis_index("dp"), lax.axis_index("z"), lax.axis_index("core")
-    coords = jnp.stack([me, plane])
+    coords = jnp.stack([me, plane, core])
     vmem = pl.BlockSpec(memory_space=pltpu.VMEM)
     smem = pl.BlockSpec(memory_space=pltpu.SMEM)
     params = pltpu.CompilerParams(vmem_limit_bytes=LIMIT)
@@ -170,9 +174,9 @@
 
     turned = jnp.transpose(grad, (0, 2, 1))
     shards = turned.shape[1]
-    near, far = (
+    far, near = (
         lax.dynamic_slice(
-            turned, (2 * lax.rem(plane + shift_of(me, j) + 2 * planes, planes), 0, 0), (2, shards, width)
+            turned, (2 * lax.rem(plane + shift_of(me, core, j) + 2 * planes, planes), 0, 0), (2, shards, width)
         )
         for j in range(2)
     )
@@ -188,10 +192,10 @@
     parts = lax.all_to_all(
         packed.reshape(2 * groups, rows // groups // 2, SIDE), ("dp", "core"), split_axis=0, concat_axis=0, tiled=True
     )
-    near, far = (
-        carry(sent, tiles, groups, planes, functools.partial(shift_of, j=j)) for j, sent in enumerate((near, far))
+    far, near = (
+        carry(sent, tiles, groups, planes, functools.partial(shift_of, j=j)) for j, sent in enumerate((far, near))
     )
-    landed = jnp.concatenate([near, far], axis=1)
+    landed = jnp.concatenate([far, near], axis=1)
     copies = pl.pallas_call(
         functools.partial(sum_kernel, total_tokens),
         out_shape=jax.ShapeDtypeStruct(
@@ -228,9 +232,8 @@
     placed = pl.pallas_call(
         place_kernel,
         out_shape=jax.ShapeDtypeStruct((tiles, shards, width), jnp.float32),
-        grid=(4,),
         in_specs=[smem, vmem],
-        out_specs=pl.BlockSpec((tiles // 4, shards, width), lambda part: (part, 0, 0)),
+        out_specs=vmem,
         compiler_params=params,
         name="place",
     )(coords, every)

time: 128 us -> 123 us (0.961)
  waiting for transfers between devices: 45.6 us -> 42.7 us
  starting transfers between devices: 66.1 us -> 64.2 us
    ppermute x4, waiting for transfers between devices: 20.1 us -> 17.2 us  [carry(): return lax.ppermute(value, ('dp', 'z', 'core'), pairs)]
    all_to_all x1, starting transfers between devices: 11.5 us -> 9.2 us  [body(): lax.all_to_all(copies, ('dp', 'core'), split_axis=0, concat_axis=0, tiled...]
  transfers between devices with their start and end apart: 7 -> 7, of which waited for: 4 -> 4; matrix products, arithmetic and copies ran while one was open for 2% -> 3% of each run, Pallas kernels for 0% -> 0%
where the time goes in v2:
time: 123 us; the launch traced here: 122 us
  starting transfers between devices  64.2 us (52%)
  waiting for transfers between devices  42.7 us (35%)
  Pallas kernels  9.28 us (8%)
  local copies, waits for them, and re-layouts  2.21 us (2%)
  between operations  2.06 us (2%)
  other arithmetic  1.8 us (1%)
    ppermute x4, starting transfers between devices, carry(): return lax.ppermute(value, ('dp', 'z', 'core'), pairs)  29.5 us
    all_to_all x1, starting transfers between devices, body(): lax.all_to_all(packed.reshape(2 * groups, rows // groups // 2, SIDE), ('d...  17.7 us
    all_to_all x1, waiting for transfers between devices, body(): lax.all_to_all(copies, ('dp', 'core'), split_axis=0, concat_axis=0, tiled...  17.6 us
    ppermute x4, waiting for transfers between devices, carry(): return lax.ppermute(value, ('dp', 'z', 'core'), pairs)  17.2 us
    all_to_all x1, starting transfers between devices, body(): lax.all_to_all(copies, ('dp', 'core'), split_axis=0, concat_axis=0, tiled...  9.2 us
    all_to_all x1, waiting for transfers between devices, spread(): lax.all_to_all(landed, ('dp', 'core'), split_axis=0, concat_axis=0, tiled...  7.92 us
    all_to_all x1, starting transfers between devices, spread(): lax.all_to_all(landed, ('dp', 'core'), split_axis=0, concat_axis=0, tiled...  7.79 us
    pallas_call x1, Pallas kernels, body(): pl.pallas_call(root_kernel, out_shape=(jax.ShapeDtypeStruct((width, width...  3.67 us
  transfers between devices with their start and end apart: 7, of which 4 were waited for; matrix products, arithmetic and copies ran while one was open for 3% of the time, Pallas kernels for 0%

profile of v2, /device:TPU:1, one launch (start us, length us, event | category | flops | bytes accessed | tf_op | source)
XLA Modules:
  0.0 122.3 jit_solution(15240340120630071932)
XLA Ops:
  0.6 2.8 %gram.1 = bf16[2560,128]{1,0:T(8,128)(2,1)} custom-call(bf16[1,512,512]{2,1,0:T(8,128)(2,1)} %acts_ref.1, bf16[1,512,512]{2,1,0:T(8,128)(2,1)} %outs_ref.1), custom_call_target="tpu_custom_call" | custom-call | tf_op jit(solution)/shard_map/gram/pallas_call | solution.py:183
  3.5 17.7 %all-to-all-start = ((bf16[32,80,128]{2,1,0:T(8,128)(2,1)}), bf16[32,80,128]{2,1,0:T(8,128)(2,1)S(1)}, u32[]{:S(2)}, u32[]{:S(2)}) async-start(bf16[32,80,128]{2,1,0:T(8,128)(2,1)} %bitcast.22), calls=%async_computation | async-start | bytes 1310720 | tf_op jit(solution)/shard_map/all_to_all | solution.py:192
  21.2 0.7 dynamic-slice_bitcast_fusion.1
  22.0 13.6 %collective-permute-start = (bf16[2,8,512]{2,1,0:T(8,128)(2,1)S(1)}, bf16[2,8,512]{2,1,0:T(8,128)(2,1)S(1)}, u32[]{:S(2)}, u32[]{:S(2)}) collective-permute-start(bf16[2,8,512]{2,1,0:T(8,128)(2,1)S(1)} %get-tuple-element.8), channel_id=1, source_target_pairs={{0,16},{1,49},{2,18},{3,51},{4,20},{5,53},{6,22},{7,55},{8,24},{9,... | collective-permute-start | bytes 49160 | tf_op jit(solution)/shard_map/ppermute | solution.py:159
  35.6 1.9 %collective-permute-start.1 = (bf16[2,8,512]{2,1,0:T(8,128)(2,1)S(1)}, bf16[2,8,512]{2,1,0:T(8,128)(2,1)S(1)}, u32[]{:S(2)}, u32[]{:S(2)}) collective-permute-start(bf16[2,8,512]{2,1,0:T(8,128)(2,1)S(1)} %get-tuple-element.9), channel_id=1, source_target_pairs={{0,48},{1,17},{2,50},{3,19},{4,52},{5,21},{6,54},{7,23},{8,56},{9,... | collective-permute-start | bytes 49160 | tf_op jit(solution)/shard_map/ppermute | solution.py:159
  37.5 0.0 collective-permute-done
  37.5 11.3 %collective-permute-done.1 = bf16[2,8,512]{2,1,0:T(8,128)(2,1)S(1)} collective-permute-done((bf16[2,8,512]{2,1,0:T(8,128)(2,1)S(1)}, bf16[2,8,512]{2,1,0:T(8,128)(2,1)S(1)}, u32[]{:S(2)}, u32[]{:S(2)}) %collective-permute-start.1) | collective-permute-done | bytes 16416 | tf_op jit(solution)/shard_map/ppermute | solution.py:159
  48.8 0.0 all-to-all-done.parts_ref
  48.8 1.2 sum.1
  49.9 9.2 %all-to-all-start.1 = ((bf16[32,144,128]{2,1,0:T(8,128)(2,1)}), bf16[32,144,128]{2,1,0:T(8,128)(2,1)S(1)}, u32[]{:S(2)}, u32[]{:S(2)}) async-start(bf16[32,144,128]{2,1,0:T(8,128)(2,1)} %sum.1), calls=%async_computation.1 | async-start | bytes 2359296 | tf_op jit(solution)/shard_map/all_to_all | solution.py:209
  59.1 0.1 pad_add_fusion.coord_ref
  59.2 17.6 %all-to-all-done.1.mixed_ref = bf16[32,144,128]{2,1,0:T(8,128)(2,1)S(1)} async-done(((bf16[32,144,128]{2,1,0:T(8,128)(2,1)}), bf16[32,144,128]{2,1,0:T(8,128)(2,1)S(1)}, u32[]{:S(2)}, u32[]{:S(2)}) %all-to-all-start.1) | async-done | bytes 1179680 | tf_op jit(solution)/shard_map/all_to_all | solution.py:209
  76.8 3.7 %roots.1 = (f32[512,512]{1,0:T(8,128)S(1)}, f32[512,512]{1,0:T(8,128)S(1)}, bf16[2,16,512]{2,1,0:T(8,128)(2,1)S(1)}) custom-call(s32[3]{0:T(128)S(1)} %pad_add_fusion.coord_ref, bf16[32,144,128]{2,1,0:T(8,128)(2,1)S(1)} %all-to-all-done.1.mixed_ref), custom_call_target="tpu_custom_call" | custom-call | tf_op jit(solution)/shard_map/roots/pallas_call | solution.py:210
  80.5 6.7 %collective-permute-start.2 = (bf16[2,8,512]{2,1,0:T(8,128)(2,1)S(1)}, bf16[2,8,512]{2,1,0:T(8,128)(2,1)S(1)}, u32[]{:S(2)}, u32[]{:S(2)}) collective-permute-start(bf16[2,8,512]{2,1,0:T(8,128)(2,1)S(1)} %get-tuple-element.10), channel_id=1, source_target_pairs={{0,16},{1,49},{2,18},{3,51},{4,20},{5,53},{6,22},{7,55},{8,24},{9,... | collective-permute-start | bytes 49160 | tf_op jit(solution)/shard_map/ppermute | solution.py:159
  87.2 7.3 %collective-permute-start.3 = (bf16[2,8,512]{2,1,0:T(8,128)(2,1)S(1)}, bf16[2,8,512]{2,1,0:T(8,128)(2,1)S(1)}, u32[]{:S(2)}, u32[]{:S(2)}) collective-permute-start(bf16[2,8,512]{2,1,0:T(8,128)(2,1)S(1)} %get-tuple-element.11), channel_id=1, source_target_pairs={{0,48},{1,17},{2,50},{3,19},{4,52},{5,21},{6,54},{7,23},{8,56},{9,... | collective-permute-start | bytes 49160 | tf_op jit(solution)/shard_map/ppermute | solution.py:159
  94.5 0.0 collective-permute-done.2
  94.5 6.0 %collective-permute-done.3 = bf16[2,8,512]{2,1,0:T(8,128)(2,1)S(1)} collective-permute-done((bf16[2,8,512]{2,1,0:T(8,128)(2,1)S(1)}, bf16[2,8,512]{2,1,0:T(8,128)(2,1)S(1)}, u32[]{:S(2)}, u32[]{:S(2)}) %collective-permute-start.3) | collective-permute-done | bytes 16416 | tf_op jit(solution)/shard_map/ppermute | solution.py:159
  100.5 0.9 broadcast_in_dim.16
  101.3 7.8 %all-to-all-start.2 = ((bf16[32,16,512]{2,1,0:T(8,128)(2,1)}), bf16[32,16,512]{2,1,0:T(8,128)(2,1)S(1)}, u32[]{:S(2)}, u32[]{:S(2)}) async-start(bf16[32,16,512]{2,1,0:T(8,128)(2,1)} %bitcast.13), calls=%async_computation.2 | async-start | bytes 1048576 | tf_op jit(solution)/shard_map/all_to_all | solution.py:149
  109.1 0.6 fusion
  111.0 0.2 select_bitcast_fusion
  111.3 1.5 %maximum_bitcast_fusion = f32[1,1,2,512,512]{4,3,2,1,0:T(8,128)} fusion(f32[1,512,512]{2,1,0:T(8,128)S(1)} %get-tuple-element.14, f32[1,512,512]{2,1,0:T(8,128)S(1)} %get-tuple-element.15), kind=kLoop, calls=%fused_computation | loop fusion | flops 524288 | bytes 4194304 | tf_op jit(solution)/shard_map/broadcast_in_dim | solution.py:223
  112.7 7.9 %all-to-all-done.2.every_ref = bf16[32,16,512]{2,1,0:T(8,128)(2,1)S(1)} async-done(((bf16[32,16,512]{2,1,0:T(8,128)(2,1)}), bf16[32,16,512]{2,1,0:T(8,128)(2,1)S(1)}, u32[]{:S(2)}, u32[]{:S(2)}) %all-to-all-start.2) | async-done | bytes 524320 | tf_op jit(solution)/shard_map/all_to_all | solution.py:149
  120.7 1.6 %place.1 = f32[64,8,512]{2,1,0:T(8,128)} custom-call(s32[3]{0:T(128)S(1)} %pad_add_fusion.coord_ref, bf16[32,16,512]{2,1,0:T(8,128)(2,1)S(1)} %all-to-all-done.2.every_ref), custom_call_target="tpu_custom_call" | custom-call | tf_op jit(solution)/shard_map/place/pallas_call | solution.py:232
  (5 shorter events, 0.0 us)
Async XLA Ops:
  3.5 45.3 %all-to-all-start = ((bf16[32,80,128]{2,1,0:T(8,128)(2,1)}), bf16[32,80,128]{2,1,0:T(8,128)(2,1)S(1)}, u32[]{:S(2)}, u32[]{:S(2)}) async-start(bf16[32,80,128]{2,1,0:T(8,128)(2,1)} %bitcast.22), calls=%async_computation | async-start | bytes 1310720 | tf_op jit(solution)/shard_map/all_to_all | solution.py:192
  22.0 15.5 %collective-permute-start = (bf16[2,8,512]{2,1,0:T(8,128)(2,1)S(1)}, bf16[2,8,512]{2,1,0:T(8,128)(2,1)S(1)}, u32[]{:S(2)}, u32[]{:S(2)}) collective-permute-start(bf16[2,8,512]{2,1,0:T(8,128)(2,1)S(1)} %get-tuple-element.8), channel_id=1, source_target_pairs={{0,16},{1,49},{2,18},{3,51},{4,20},{5,53},{6,22},{7,55},{8,24},{9,... | collective-permute-start | bytes 49160 | tf_op jit(solution)/shard_map/ppermute | solution.py:159
  35.6 13.2 %collective-permute-start.1 = (bf16[2,8,512]{2,1,0:T(8,128)(2,1)S(1)}, bf16[2,8,512]{2,1,0:T(8,128)(2,1)S(1)}, u32[]{:S(2)}, u32[]{:S(2)}) collective-permute-start(bf16[2,8,512]{2,1,0:T(8,128)(2,1)S(1)} %get-tuple-element.9), channel_id=1, source_target_pairs={{0,48},{1,17},{2,50},{3,19},{4,52},{5,21},{6,54},{7,23},{8,56},{9,... | collective-permute-start | bytes 49160 | tf_op jit(solution)/shard_map/ppermute | solution.py:159
  49.9 59.2 %copy-start = (s32[1,2]{1,0:T(1,128)S(1)}, s32[1,2]{1,0:T(1,128)}, u32[]{:S(2)}) copy-start(s32[1,2]{1,0:T(1,128)} %param.7) | copy-start | bytes 28
  49.9 26.9 %all-to-all-start.1 = ((bf16[32,144,128]{2,1,0:T(8,128)(2,1)}), bf16[32,144,128]{2,1,0:T(8,128)(2,1)S(1)}, u32[]{:S(2)}, u32[]{:S(2)}) async-start(bf16[32,144,128]{2,1,0:T(8,128)(2,1)} %sum.1), calls=%async_computation.1 | async-start | bytes 2359296 | tf_op jit(solution)/shard_map/all_to_all | solution.py:209
  80.5 14.0 %collective-permute-start.2 = (bf16[2,8,512]{2,1,0:T(8,128)(2,1)S(1)}, bf16[2,8,512]{2,1,0:T(8,128)(2,1)S(1)}, u32[]{:S(2)}, u32[]{:S(2)}) collective-permute-start(bf16[2,8,512]{2,1,0:T(8,128)(2,1)S(1)} %get-tuple-element.10), channel_id=1, source_target_pairs={{0,16},{1,49},{2,18},{3,51},{4,20},{5,53},{6,22},{7,55},{8,24},{9,... | collective-permute-start | bytes 49160 | tf_op jit(solution)/shard_map/ppermute | solution.py:159
  87.2 13.3 %collective-permute-start.3 = (bf16[2,8,512]{2,1,0:T(8,128)(2,1)S(1)}, bf16[2,8,512]{2,1,0:T(8,128)(2,1)S(1)}, u32[]{:S(2)}, u32[]{:S(2)}) collective-permute-start(bf16[2,8,512]{2,1,0:T(8,128)(2,1)S(1)} %get-tuple-element.11), channel_id=1, source_target_pairs={{0,48},{1,17},{2,50},{3,19},{4,52},{5,21},{6,54},{7,23},{8,56},{9,... | collective-permute-start | bytes 49160 | tf_op jit(solution)/shard_map/ppermute | solution.py:159
  101.3 19.3 %all-to-all-start.2 = ((bf16[32,16,512]{2,1,0:T(8,128)(2,1)}), bf16[32,16,512]{2,1,0:T(8,128)(2,1)S(1)}, u32[]{:S(2)}, u32[]{:S(2)}) async-start(bf16[32,16,512]{2,1,0:T(8,128)(2,1)} %bitcast.13), calls=%async_computation.2 | async-start | bytes 1048576 | tf_op jit(solution)/shard_map/all_to_all | solution.py:149

commit v3 on v2

--- a/solution.py
+++ b/solution.py
@@ -17,7 +17,7 @@
     return [(i, j) for i in range(n) for j in range(i, n)]
 
 
-def gram_kernel(acts_ref, outs_ref, packed_ref, held_ref, sems):
+def gram_kernel(coord_ref, acts_ref, outs_ref, grad_ref, packed_ref, far_ref, near_ref, held_ref, sems, grad_sems):
     tokens, width = acts_ref.shape[1:]
     places = blocks(width)
     wide = 2 * SIDE
@@ -27,6 +27,13 @@
             span = pl.ds(part * (tokens // 2), tokens // 2)
             copies.append(pltpu.make_async_copy(ref.at[0, span], held_ref.at[which, span], sems.at[which, part]))
             copies[-1].start()
+    me, plane, core = coord_ref[0], coord_ref[1], coord_ref[2]
+    planes = grad_ref.shape[0] // 2
+    shards = []
+    for j, ref in enumerate((far_ref, near_ref)):
+        goal = lax.rem(plane + shift_of(me, core, j) + 2 * planes, planes)
+        shards.append(pltpu.make_async_copy(grad_ref.at[pl.ds(2 * goal, 2)], ref, grad_sems.at[j]))
+        shards[-1].start()
     for which in range(2):
         base = which * len(places)
         copies[2 * which].wait()
@@ -42,6 +49,8 @@
                     packed_ref[pl.ds((base + spot) * SIDE, SIDE), :] = part[
                         row : row + SIDE, col : col + SIDE
                     ].astype(packed_ref.dtype)
+    for copy in shards:
+        copy.wait()
 
 
 def sum_kernel(total_tokens, parts_ref, shards_ref, copies_ref):
@@ -121,25 +130,33 @@
         piece_ref[j] = product[j * tall : (j + 1) * tall]
 
 
-def place_kernel(coord_ref, every_ref, out_ref):
+def place_kernel(coord_ref, every_ref, out_ref, held_ref, sem):
     plane = coord_ref[1]
     planes = every_ref.shape[0]
     half = every_ref.shape[1] // 2
-    for i in range(planes):
-        block = every_ref[i].astype(jnp.float32)
-        for j in range(2):
-            source = lax.rem(plane - shift_of(i // 2, i % 2, j) + 2 * planes, planes)
-            out_ref[2 * source + i % 2] = block[j * half : (j + 1) * half]
+    for shift in range(planes):
+        source = lax.rem(plane - shift + planes, planes)
+        for core in range(2):
+            d, j = holder_of(shift, core)
+            block = every_ref[2 * d + core].astype(jnp.float32)
+            held_ref[2 * source + core] = block[j * half : (j + 1) * half]
+        span = pl.ds(2 * source, 2)
+        pltpu.make_async_copy(held_ref.at[span], out_ref.at[span], sem).start()
+    pltpu.make_async_copy(held_ref, out_ref, sem).wait()
+
+
+def seat_of(d, core):
+    return d + core * (d % 8 == 0) * (8 - 2 * d)
 
 
 def shift_of(d, core, j):
-    ahead = d + 8 if j == 0 else d - 8
-    return ahead * (1 - 2 * core)
+    seat = seat_of(d, core)
+    return (seat + 8 if j == 0 else seat - 8) * (1 - 2 * core)
 
 
 def holder_of(shift, core):
     turn = ((1 - 2 * core) * shift + 8) % 32
-    return turn % 16, 1 - turn // 16
+    return seat_of(turn % 16, core), 1 - turn // 16
 
 
 def spread(far, near, groups):
@@ -174,21 +191,20 @@
 
     turned = jnp.transpose(grad, (0, 2, 1))
     shards = turned.shape[1]
-    far, near = (
-        lax.dynamic_slice(
-            turned, (2 * lax.rem(plane + shift_of(me, core, j) + 2 * planes, planes), 0, 0), (2, shards, width)
-        )
-        for j in range(2)
-    )
-    packed = pl.pallas_call(
+    shard = jax.ShapeDtypeStruct((2, shards, width), grad.dtype)
+    packed, far, near = pl.pallas_call(
         gram_kernel,
-        out_shape=jax.ShapeDtypeStruct((rows, SIDE), jnp.bfloat16),
-        in_specs=[pl.BlockSpec(memory_space=pl.ANY)] * 2,
-        out_specs=vmem,
-        scratch_shapes=[pltpu.VMEM((2,) + acts.shape[1:], acts.dtype), pltpu.SemaphoreType.DMA((2, 2))],
+        out_shape=(jax.ShapeDtypeStruct((rows, SIDE), jnp.bfloat16), shard, shard),
+        in_specs=[smem] + [pl.BlockSpec(memory_space=pl.ANY)] * 3,
+        out_specs=(vmem, vmem, vmem),
+        scratch_shapes=[
+            pltpu.VMEM((2,) + acts.shape[1:], acts.dtype),
+            pltpu.SemaphoreType.DMA((2, 2)),
+            pltpu.SemaphoreType.DMA((2,)),
+        ],
         compiler_params=pltpu.CompilerParams(vmem_limit_bytes=60 * 1024 * 1024),
         name="gram",
-    )(acts, outgrads)
+    )(coords, acts, outgrads, turned)
     parts = lax.all_to_all(
         packed.reshape(2 * groups, rows // groups // 2, SIDE), ("dp", "core"), split_axis=0, concat_axis=0, tiled=True
     )
@@ -233,7 +249,8 @@
         place_kernel,
         out_shape=jax.ShapeDtypeStruct((tiles, shards, width), jnp.float32),
         in_specs=[smem, vmem],
-        out_specs=vmem,
+        out_specs=pl.BlockSpec(memory_space=pl.ANY),
+        scratch_shapes=[pltpu.VMEM((tiles, shards, width), jnp.float32), pltpu.SemaphoreType.DMA],
         compiler_params=params,
         name="place",
     )(coords, every)

time: 123 us -> 123 us (level)
  blocking collectives: 0 us -> 31.7 us
  waiting for transfers between devices: 42.7 us -> 19.5 us
  starting transfers between devices: 64.2 us -> 56.2 us
    all_to_all x0 -> x1, blocking collectives: none -> 31.7 us  [body(): lax.all_to_all(copies, ('dp', 'core'), split_axis=0, concat_axis=0, tiled...]
    all_to_all x1 -> x0, waiting for transfers between devices: 17.6 us -> none  [body(): lax.all_to_all(copies, ('dp', 'core'), split_axis=0, concat_axis=0, tiled...]
    all_to_all x1 -> x0, starting transfers between devices: 9.2 us -> none  [body(): lax.all_to_all(copies, ('dp', 'core'), split_axis=0, concat_axis=0, tiled...]
    ppermute x4, waiting for transfers between devices: 17.2 us -> 11.5 us  [carry(): return lax.ppermute(value, ('dp', 'z', 'core'), pairs)]
    ppermute x4, starting transfers between devices: 29.5 us -> 34.3 us  [carry(): return lax.ppermute(value, ('dp', 'z', 'core'), pairs)]
    all_to_all x1, starting transfers between devices: 7.79 us -> 4.23 us  [spread(): lax.all_to_all(landed, ('dp', 'core'), split_axis=0, concat_axis=0, tiled...]
  transfers between devices with their start and end apart: 7 -> 6, of which waited for: 4 -> 3; matrix products, arithmetic and copies ran while one was open for 3% -> 2% of each run, Pallas kernels for 0% -> 0%
where the time goes in v3:
time: 123 us; the launch traced here: 122 us
  starting transfers between devices  56.2 us (46%)
  blocking collectives  31.7 us (26%)
  waiting for transfers between devices  19.5 us (16%)
  Pallas kernels  8.8 us (7%)
  other arithmetic  2.33 us (2%)
  between operations  2.03 us (2%)
  local copies, waits for them, and re-layouts  1.49 us (1%)
    ppermute x4, starting transfers between devices, carry(): return lax.ppermute(value, ('dp', 'z', 'core'), pairs)  34.3 us
    all_to_all x1, blocking collectives, body(): lax.all_to_all(copies, ('dp', 'core'), split_axis=0, concat_axis=0, tiled...  31.7 us
    all_to_all x1, starting transfers between devices, body(): lax.all_to_all(packed.reshape(2 * groups, rows // groups // 2, SIDE), ('d...  17.7 us
    ppermute x4, waiting for transfers between devices, carry(): return lax.ppermute(value, ('dp', 'z', 'core'), pairs)  11.5 us
    all_to_all x1, waiting for transfers between devices, spread(): lax.all_to_all(landed, ('dp', 'core'), split_axis=0, concat_axis=0, tiled...  7.91 us
    all_to_all x1, starting transfers between devices, spread(): lax.all_to_all(landed, ('dp', 'core'), split_axis=0, concat_axis=0, tiled...  4.23 us
    pallas_call x1, Pallas kernels, body(): pl.pallas_call(root_kernel, out_shape=(jax.ShapeDtypeStruct((width, width...  3.65 us
    pallas_call x1, Pallas kernels, body(): pl.pallas_call(gram_kernel, out_shape=(jax.ShapeDtypeStruct((rows, SIDE),...  3.51 us
  transfers between devices with their start and end apart: 6, of which 3 were waited for; matrix products, arithmetic and copies ran while one was open for 2% of the time, Pallas kernels for 0%

profile of v3, /device:TPU:1, one launch (start us, length us, event | category | flops | bytes accessed | tf_op | source)
XLA Modules:
  0.0 122.0 jit_solution(15551271251375682741)
XLA Ops:
  0.6 0.6 pad_add_fusion.coord_ref
  1.2 3.5 %gram.1 = (bf16[2560,128]{1,0:T(8,128)(2,1)}, bf16[2,8,512]{2,1,0:T(8,128)(2,1)}, bf16[2,8,512]{2,1,0:T(8,128)(2,1)}) custom-call(s32[3]{0:T(128)} %pad_add_fusion.coord_ref, bf16[1,512,512]{2,1,0:T(8,128)(2,1)} %acts_ref.1, bf16[1,512,512]{2,1,0:T(8,128)(2,1)} %outs_ref.1, bf16[64,8,512]{2,1,0:T(8,128)(2,1)} %bitcast.21), custom_call_target="tpu_custom_call" | custom-call | tf_op jit(solution)/shard_map/gram/pallas_call | solution.py:195
  4.8 17.7 %all-to-all-start = ((bf16[32,80,128]{2,1,0:T(8,128)(2,1)}), bf16[32,80,128]{2,1,0:T(8,128)(2,1)S(1)}, u32[]{:S(2)}, u32[]{:S(2)}) async-start(bf16[32,80,128]{2,1,0:T(8,128)(2,1)} %bitcast.20), calls=%async_computation | async-start | bytes 1310720 | tf_op jit(solution)/shard_map/all_to_all | solution.py:208
  22.5 19.6 %collective-permute-start = (bf16[2,8,512]{2,1,0:T(8,128)(2,1)}, bf16[2,8,512]{2,1,0:T(8,128)(2,1)S(1)}, u32[]{:S(2)}, u32[]{:S(2)}) collective-permute-start(bf16[2,8,512]{2,1,0:T(8,128)(2,1)} %get-tuple-element.9), channel_id=1, source_target_pairs={{0,16},{1,33},{2,18},{3,35},{4,20},{5,37},{6,22},{7,39},{8,24},{9,... | collective-permute-start | bytes 49160 | tf_op jit(solution)/shard_map/ppermute | solution.py:176
  42.1 1.4 %collective-permute-start.1 = (bf16[2,8,512]{2,1,0:T(8,128)(2,1)}, bf16[2,8,512]{2,1,0:T(8,128)(2,1)S(1)}, u32[]{:S(2)}, u32[]{:S(2)}) collective-permute-start(bf16[2,8,512]{2,1,0:T(8,128)(2,1)} %get-tuple-element.10), channel_id=1, source_target_pairs={{0,48},{1,1},{2,50},{3,3},{4,52},{5,5},{6,54},{7,7},{8,56},{9,9},{... | collective-permute-start | bytes 49160 | tf_op jit(solution)/shard_map/ppermute | solution.py:176
  43.5 2.1 %collective-permute-done = bf16[2,8,512]{2,1,0:T(8,128)(2,1)S(1)} collective-permute-done((bf16[2,8,512]{2,1,0:T(8,128)(2,1)}, bf16[2,8,512]{2,1,0:T(8,128)(2,1)S(1)}, u32[]{:S(2)}, u32[]{:S(2)}) %collective-permute-start) | collective-permute-done | bytes 16416 | tf_op jit(solution)/shard_map/ppermute | solution.py:176
  45.5 0.0 collective-permute-done.1
  45.5 0.0 all-to-all-done.parts_ref
  45.5 0.1 sum.1
  45.7 0.0 copy-start.1
  45.7 31.7 %all_to_all.15.mixed_ref = bf16[32,144,128]{2,1,0:T(8,128)(2,1)S(1)} all-to-all(bf16[32,144,128]{2,1,0:T(8,128)(2,1)S(1)} %sum.1), channel_id=1, replica_groups=mesh['dp'=16,'z'=32,'core'=2] {'dp','core'}, dimensions={0} | all-to-all | bytes 2359296 | tf_op jit(solution)/shard_map/all_to_all | solution.py:225
  77.4 0.0 copy-done
  77.4 3.6 %roots.1 = (f32[512,512]{1,0:T(8,128)S(1)}, f32[512,512]{1,0:T(8,128)S(1)}, bf16[2,16,512]{2,1,0:T(8,128)(2,1)S(1)}) custom-call(s32[3]{0:T(128)S(1)} %copy-done, bf16[32,144,128]{2,1,0:T(8,128)(2,1)S(1)} %all_to_all.15.mixed_ref), custom_call_target="tpu_custom_call" | custom-call | tf_op jit(solution)/shard_map/roots/pallas_call | solution.py:226
  81.1 12.7 %collective-permute-start.2 = (bf16[2,8,512]{2,1,0:T(8,128)(2,1)S(1)}, bf16[2,8,512]{2,1,0:T(8,128)(2,1)S(1)}, u32[]{:S(2)}, u32[]{:S(2)}) collective-permute-start(bf16[2,8,512]{2,1,0:T(8,128)(2,1)S(1)} %get-tuple-element.14), channel_id=1, source_target_pairs={{0,16},{1,33},{2,18},{3,35},{4,20},{5,37},{6,22},{7,39},{8,24},{9,... | collective-permute-start | bytes 49160 | tf_op jit(solution)/shard_map/ppermute | solution.py:176
  93.7 0.7 collective-permute-start.3
  94.4 9.5 %collective-permute-done.2 = bf16[2,8,512]{2,1,0:T(8,128)(2,1)S(1)} collective-permute-done((bf16[2,8,512]{2,1,0:T(8,128)(2,1)S(1)}, bf16[2,8,512]{2,1,0:T(8,128)(2,1)S(1)}, u32[]{:S(2)}, u32[]{:S(2)}) %collective-permute-start.2) | collective-permute-done | bytes 16416 | tf_op jit(solution)/shard_map/ppermute | solution.py:176
  103.9 0.0 collective-permute-done.3
  103.9 0.9 broadcast_in_dim.16
  104.7 4.2 %all-to-all-start.2 = ((bf16[32,16,512]{2,1,0:T(8,128)(2,1)}), bf16[32,16,512]{2,1,0:T(8,128)(2,1)S(1)}, u32[]{:S(2)}, u32[]{:S(2)}) async-start(bf16[32,16,512]{2,1,0:T(8,128)(2,1)} %bitcast.12), calls=%async_computation.2 | async-start | bytes 1048576 | tf_op jit(solution)/shard_map/all_to_all | solution.py:166
  109.0 0.6 fusion
  110.9 0.2 select_bitcast_fusion
  111.1 1.5 %maximum_bitcast_fusion = f32[1,1,2,512,512]{4,3,2,1,0:T(8,128)} fusion(f32[1,512,512]{2,1,0:T(8,128)S(1)} %get-tuple-element.18, f32[1,512,512]{2,1,0:T(8,128)S(1)} %get-tuple-element.19), kind=kLoop, calls=%fused_computation | loop fusion | flops 524288 | bytes 4194304 | tf_op jit(solution)/shard_map/broadcast_in_dim | solution.py:239
  112.6 7.9 %all-to-all-done.2.every_ref = bf16[32,16,512]{2,1,0:T(8,128)(2,1)S(1)} async-done(((bf16[32,16,512]{2,1,0:T(8,128)(2,1)}), bf16[32,16,512]{2,1,0:T(8,128)(2,1)S(1)}, u32[]{:S(2)}, u32[]{:S(2)}) %all-to-all-start.2) | async-done | bytes 524320 | tf_op jit(solution)/shard_map/all_to_all | solution.py:166
  120.5 1.5 %place.1 = f32[64,8,512]{2,1,0:T(8,128)} custom-call(s32[3]{0:T(128)S(1)} %copy-done, bf16[32,16,512]{2,1,0:T(8,128)(2,1)S(1)} %all-to-all-done.2.every_ref), custom_call_target="tpu_custom_call" | custom-call | tf_op jit(solution)/shard_map/place/pallas_call | solution.py:248
  (5 shorter events, 0.0 us)
Async XLA Ops:
  4.8 40.8 %all-to-all-start = ((bf16[32,80,128]{2,1,0:T(8,128)(2,1)}), bf16[32,80,128]{2,1,0:T(8,128)(2,1)S(1)}, u32[]{:S(2)}, u32[]{:S(2)}) async-start(bf16[32,80,128]{2,1,0:T(8,128)(2,1)} %bitcast.20), calls=%async_computation | async-start | bytes 1310720 | tf_op jit(solution)/shard_map/all_to_all | solution.py:208
  22.5 23.0 %collective-permute-start = (bf16[2,8,512]{2,1,0:T(8,128)(2,1)}, bf16[2,8,512]{2,1,0:T(8,128)(2,1)S(1)}, u32[]{:S(2)}, u32[]{:S(2)}) collective-permute-start(bf16[2,8,512]{2,1,0:T(8,128)(2,1)} %get-tuple-element.9), channel_id=1, source_target_pairs={{0,16},{1,33},{2,18},{3,35},{4,20},{5,37},{6,22},{7,39},{8,24},{9,... | collective-permute-start | bytes 49160 | tf_op jit(solution)/shard_map/ppermute | solution.py:176
  42.1 3.4 %collective-permute-start.1 = (bf16[2,8,512]{2,1,0:T(8,128)(2,1)}, bf16[2,8,512]{2,1,0:T(8,128)(2,1)S(1)}, u32[]{:S(2)}, u32[]{:S(2)}) collective-permute-start(bf16[2,8,512]{2,1,0:T(8,128)(2,1)} %get-tuple-element.10), channel_id=1, source_target_pairs={{0,48},{1,1},{2,50},{3,3},{4,52},{5,5},{6,54},{7,7},{8,56},{9,9},{... | collective-permute-start | bytes 49160 | tf_op jit(solution)/shard_map/ppermute | solution.py:176
  45.5 31.9 %copy-start = (s32[3]{0:T(128)S(1)}, s32[3]{0:T(128)}, u32[]{:S(2)}) copy-start(s32[3]{0:T(128)} %pad_add_fusion.coord_ref) | copy-start | bytes 40
  45.7 63.3 %copy-start.1 = (s32[1,2]{1,0:T(1,128)S(1)}, s32[1,2]{1,0:T(1,128)}, u32[]{:S(2)}) copy-start(s32[1,2]{1,0:T(1,128)} %param.7) | copy-start | bytes 28
  81.1 22.8 %collective-permute-start.2 = (bf16[2,8,512]{2,1,0:T(8,128)(2,1)S(1)}, bf16[2,8,512]{2,1,0:T(8,128)(2,1)S(1)}, u32[]{:S(2)}, u32[]{:S(2)}) collective-permute-start(bf16[2,8,512]{2,1,0:T(8,128)(2,1)S(1)} %get-tuple-element.14), channel_id=1, source_target_pairs={{0,16},{1,33},{2,18},{3,35},{4,20},{5,37},{6,22},{7,39},{8,24},{9,... | collective-permute-start | bytes 49160 | tf_op jit(solution)/shard_map/ppermute | solution.py:176
  93.7 10.1 %collective-permute-start.3 = (bf16[2,8,512]{2,1,0:T(8,128)(2,1)S(1)}, bf16[2,8,512]{2,1,0:T(8,128)(2,1)S(1)}, u32[]{:S(2)}, u32[]{:S(2)}) collective-permute-start(bf16[2,8,512]{2,1,0:T(8,128)(2,1)S(1)} %get-tuple-element.15), channel_id=1, source_target_pairs={{0,48},{1,1},{2,50},{3,3},{4,52},{5,5},{6,54},{7,7},{8,56},{9,9},{... | collective-permute-start | bytes 49160 | tf_op jit(solution)/shard_map/ppermute | solution.py:176
  104.7 15.8 %all-to-all-start.2 = ((bf16[32,16,512]{2,1,0:T(8,128)(2,1)}), bf16[32,16,512]{2,1,0:T(8,128)(2,1)S(1)}, u32[]{:S(2)}, u32[]{:S(2)}) async-start(bf16[32,16,512]{2,1,0:T(8,128)(2,1)} %bitcast.12), calls=%async_computation.2 | async-start | bytes 1048576 | tf_op jit(solution)/shard_map/all_to_all | solution.py:166

commit v4 on v2

--- a/solution.py
+++ b/solution.py
@@ -121,32 +121,52 @@
         piece_ref[j] = product[j * tall : (j + 1) * tall]
 
 
-def place_kernel(coord_ref, every_ref, out_ref):
+def place_kernel(coord_ref, every_ref, out_ref, held_ref, sem):
     plane = coord_ref[1]
     planes = every_ref.shape[0]
     half = every_ref.shape[1] // 2
-    for i in range(planes):
-        block = every_ref[i].astype(jnp.float32)
-        for j in range(2):
-            source = lax.rem(plane - shift_of(i // 2, i % 2, j) + 2 * planes, planes)
-            out_ref[2 * source + i % 2] = block[j * half : (j + 1) * half]
+    for shift in range(planes):
+        source = lax.rem(plane - shift + planes, planes)
+        for core in range(2):
+            d, j = holder_of(shift, core)
+            block = every_ref[2 * d + core].astype(jnp.float32)
+            held_ref[2 * source + core] = block[j * half : (j + 1) * half]
+        span = pl.ds(2 * source, 2)
+        pltpu.make_async_copy(held_ref.at[span], out_ref.at[span], sem).start()
+    pltpu.make_async_copy(held_ref, out_ref, sem).wait()
+
+
+def seat_of(d, core):
+    return d + core * (d % 8 == 0) * (8 - 2 * d)
 
 
 def shift_of(d, core, j):
-    ahead = d + 8 if j == 0 else d - 8
-    return ahead * (1 - 2 * core)
+    seat = seat_of(d, core)
+    return (seat + 8 if j == 0 else seat - 8) * (1 - 2 * core)
 
 
 def holder_of(shift, core):
     turn = ((1 - 2 * core) * shift + 8) % 32
-    return turn % 16, 1 - turn // 16
-
-
-def spread(far, near, groups):
+    return seat_of(turn % 16, core), 1 - turn // 16
+
+
+def fan_kernel(landed_ref, copies_ref):
+    for g in range(copies_ref.shape[0]):
+        copies_ref[g] = landed_ref[g % 2]
+
+
+def spread(far, near, groups, params):
     landed = jnp.concatenate([far, near], axis=1)
-    landed = jnp.broadcast_to(landed[None], (groups,) + landed.shape)
-    landed = landed.reshape((-1,) + landed.shape[2:])
-    return lax.all_to_all(landed, ("dp", "core"), split_axis=0, concat_axis=0, tiled=True)
+    vmem = pl.BlockSpec(memory_space=pltpu.VMEM)
+    copies = pl.pallas_call(
+        fan_kernel,
+        out_shape=jax.ShapeDtypeStruct((2 * groups,) + landed.shape[1:], landed.dtype),
+        in_specs=[vmem],
+        out_specs=vmem,
+        compiler_params=params,
+        name="fan",
+    )(landed)
+    return lax.all_to_all(copies, ("dp", "core"), split_axis=0, concat_axis=0, tiled=True)
 
 
 def carry(value, tiles, groups, planes, shift):
@@ -228,12 +248,13 @@
         carry(piece[j].reshape(2, shards, width), tiles, groups, planes, functools.partial(shift_of, j=j))
         for j in range(2)
     ]
-    every = spread(*landed, groups)
+    every = spread(*landed, groups, params)
     placed = pl.pallas_call(
         place_kernel,
         out_shape=jax.ShapeDtypeStruct((tiles, shards, width), jnp.float32),
         in_specs=[smem, vmem],
-        out_specs=vmem,
+        out_specs=pl.BlockSpec(memory_space=pl.ANY),
+        scratch_shapes=[pltpu.VMEM((tiles, shards, width), jnp.float32), pltpu.SemaphoreType.DMA],
         compiler_params=params,
         name="place",
     )(coords, every)

time: 123 us -> 123 us (level)
  waiting for transfers between devices: 42.7 us -> 37.6 us
  starting transfers between devices: 64.2 us -> 69.3 us
    ppermute x4, waiting for transfers between devices: 17.2 us -> 12.1 us  [carry(): return lax.ppermute(value, ('dp', 'z', 'core'), pairs)]
    ppermute x4, starting transfers between devices: 29.5 us -> 33.5 us  [carry(): return lax.ppermute(value, ('dp', 'z', 'core'), pairs)]
    all_to_all x1, starting transfers between devices: 9.2 us -> 13.2 us  [body(): lax.all_to_all(copies, ('dp', 'core'), split_axis=0, concat_axis=0, tiled...]
    all_to_all x1, starting transfers between devices: 7.79 us -> 4.89 us  [spread(): lax.all_to_all(copies, ('dp', 'core'), split_axis=0, concat_axis=0, tiled...]
where the time goes in v4:
time: 123 us; the launch traced here: 122 us
  starting transfers between devices  69.3 us (56%)
  waiting for transfers between devices  37.6 us (31%)
  Pallas kernels  9.95 us (8%)
  between operations  2.06 us (2%)
  other arithmetic  1.8 us (1%)
  local copies, waits for them, and re-layouts  1.36 us (1%)
    ppermute x4, starting transfers between devices, carry(): return lax.ppermute(value, ('dp', 'z', 'core'), pairs)  33.5 us
    all_to_all x1, starting transfers between devices, body(): lax.all_to_all(packed.reshape(2 * groups, rows // groups // 2, SIDE), ('d...  17.7 us
    all_to_all x1, waiting for transfers between devices, body(): lax.all_to_all(copies, ('dp', 'core'), split_axis=0, concat_axis=0, tiled...  17.6 us
    all_to_all x1, starting transfers between devices, body(): lax.all_to_all(copies, ('dp', 'core'), split_axis=0, concat_axis=0, tiled...  13.2 us
    ppermute x4, waiting for transfers between devices, carry(): return lax.ppermute(value, ('dp', 'z', 'core'), pairs)  12.1 us
    all_to_all x1, waiting for transfers between devices, spread(): lax.all_to_all(copies, ('dp', 'core'), split_axis=0, concat_axis=0, tiled...  7.92 us
    all_to_all x1, starting transfers between devices, spread(): lax.all_to_all(copies, ('dp', 'core'), split_axis=0, concat_axis=0, tiled...  4.89 us
    pallas_call x1, Pallas kernels, body(): pl.pallas_call(root_kernel, out_shape=(jax.ShapeDtypeStruct((width, width...  3.63 us
  transfers between devices with their start and end apart: 7, of which 4 were waited for; matrix products, arithmetic and copies ran while one was open for 3% of the time, Pallas kernels for 0%

profile of v4, /device:TPU:1, one launch (start us, length us, event | category | flops | bytes accessed | tf_op | source)
XLA Modules:
  0.0 122.1 jit_solution(2109230750447170485)
XLA Ops:
  0.6 2.8 %gram.1 = bf16[2560,128]{1,0:T(8,128)(2,1)} custom-call(bf16[1,512,512]{2,1,0:T(8,128)(2,1)} %acts_ref.1, bf16[1,512,512]{2,1,0:T(8,128)(2,1)} %outs_ref.1), custom_call_target="tpu_custom_call" | custom-call | tf_op jit(solution)/shard_map/gram/pallas_call | solution.py:203
  3.5 17.7 %all-to-all-start = ((bf16[32,80,128]{2,1,0:T(8,128)(2,1)}), bf16[32,80,128]{2,1,0:T(8,128)(2,1)S(1)}, u32[]{:S(2)}, u32[]{:S(2)}) async-start(bf16[32,80,128]{2,1,0:T(8,128)(2,1)} %bitcast.21), calls=%async_computation | async-start | bytes 1310720 | tf_op jit(solution)/shard_map/all_to_all | solution.py:212
  21.2 0.7 dynamic-slice_bitcast_fusion.1
  22.0 19.6 %collective-permute-start = (bf16[2,8,512]{2,1,0:T(8,128)(2,1)S(1)}, bf16[2,8,512]{2,1,0:T(8,128)(2,1)S(1)}, u32[]{:S(2)}, u32[]{:S(2)}) collective-permute-start(bf16[2,8,512]{2,1,0:T(8,128)(2,1)S(1)} %get-tuple-element.8), channel_id=1, source_target_pairs={{0,16},{1,33},{2,18},{3,35},{4,20},{5,37},{6,22},{7,39},{8,24},{9,... | collective-permute-start | bytes 49160 | tf_op jit(solution)/shard_map/ppermute | solution.py:179
  41.5 0.7 collective-permute-start.1
  42.2 2.6 %collective-permute-done = bf16[2,8,512]{2,1,0:T(8,128)(2,1)S(1)} collective-permute-done((bf16[2,8,512]{2,1,0:T(8,128)(2,1)S(1)}, bf16[2,8,512]{2,1,0:T(8,128)(2,1)S(1)}, u32[]{:S(2)}, u32[]{:S(2)}) %collective-permute-start) | collective-permute-done | bytes 16416 | tf_op jit(solution)/shard_map/ppermute | solution.py:179
  44.8 0.0 collective-permute-done.1
  44.8 0.0 all-to-all-done.parts_ref
  44.8 1.2 sum.1
  45.9 13.2 %all-to-all-start.1 = ((bf16[32,144,128]{2,1,0:T(8,128)(2,1)}), bf16[32,144,128]{2,1,0:T(8,128)(2,1)S(1)}, u32[]{:S(2)}, u32[]{:S(2)}) async-start(bf16[32,144,128]{2,1,0:T(8,128)(2,1)} %sum.1), calls=%async_computation.1 | async-start | bytes 2359296 | tf_op jit(solution)/shard_map/all_to_all | solution.py:229
  59.1 0.1 pad_add_fusion.coord_ref
  59.2 17.6 %all-to-all-done.1.mixed_ref = bf16[32,144,128]{2,1,0:T(8,128)(2,1)S(1)} async-done(((bf16[32,144,128]{2,1,0:T(8,128)(2,1)}), bf16[32,144,128]{2,1,0:T(8,128)(2,1)S(1)}, u32[]{:S(2)}, u32[]{:S(2)}) %all-to-all-start.1) | async-done | bytes 1179680 | tf_op jit(solution)/shard_map/all_to_all | solution.py:229
  76.8 3.6 %roots.1 = (f32[512,512]{1,0:T(8,128)S(1)}, f32[512,512]{1,0:T(8,128)S(1)}, bf16[2,16,512]{2,1,0:T(8,128)(2,1)S(1)}) custom-call(s32[3]{0:T(128)S(1)} %pad_add_fusion.coord_ref, bf16[32,144,128]{2,1,0:T(8,128)(2,1)S(1)} %all-to-all-done.1.mixed_ref), custom_call_target="tpu_custom_call" | custom-call | tf_op jit(solution)/shard_map/roots/pallas_call | solution.py:230
  80.5 12.6 %collective-permute-start.2 = (bf16[2,8,512]{2,1,0:T(8,128)(2,1)S(1)}, bf16[2,8,512]{2,1,0:T(8,128)(2,1)S(1)}, u32[]{:S(2)}, u32[]{:S(2)}) collective-permute-start(bf16[2,8,512]{2,1,0:T(8,128)(2,1)S(1)} %get-tuple-element.10), channel_id=1, source_target_pairs={{0,16},{1,33},{2,18},{3,35},{4,20},{5,37},{6,22},{7,39},{8,24},{9,... | collective-permute-start | bytes 49160 | tf_op jit(solution)/shard_map/ppermute | solution.py:179
  93.1 0.7 collective-permute-start.3
  93.8 9.5 %collective-permute-done.2 = bf16[2,8,512]{2,1,0:T(8,128)(2,1)S(1)} collective-permute-done((bf16[2,8,512]{2,1,0:T(8,128)(2,1)S(1)}, bf16[2,8,512]{2,1,0:T(8,128)(2,1)S(1)}, u32[]{:S(2)}, u32[]{:S(2)}) %collective-permute-start.2) | collective-permute-done | bytes 16416 | tf_op jit(solution)/shard_map/ppermute | solution.py:179
  103.3 0.0 collective-permute-done.3
  103.3 0.8 fan.1
  104.2 4.9 %all-to-all-start.2 = ((bf16[32,16,512]{2,1,0:T(8,128)(2,1)}), bf16[32,16,512]{2,1,0:T(8,128)(2,1)S(1)}, u32[]{:S(2)}, u32[]{:S(2)}) async-start(bf16[32,16,512]{2,1,0:T(8,128)(2,1)} %fan.1), calls=%async_computation.2 | async-start | bytes 1048576 | tf_op jit(solution)/shard_map/all_to_all | solution.py:169
  109.1 0.6 fusion
  111.0 0.2 select_bitcast_fusion
  111.2 1.5 %maximum_bitcast_fusion = f32[1,1,2,512,512]{4,3,2,1,0:T(8,128)} fusion(f32[1,512,512]{2,1,0:T(8,128)S(1)} %get-tuple-element.14, f32[1,512,512]{2,1,0:T(8,128)S(1)} %get-tuple-element.15), kind=kLoop, calls=%fused_computation | loop fusion | flops 524288 | bytes 4194304 | tf_op jit(solution)/shard_map/broadcast_in_dim | solution.py:243
  112.7 7.9 %all-to-all-done.2.every_ref = bf16[32,16,512]{2,1,0:T(8,128)(2,1)S(1)} async-done(((bf16[32,16,512]{2,1,0:T(8,128)(2,1)}), bf16[32,16,512]{2,1,0:T(8,128)(2,1)S(1)}, u32[]{:S(2)}, u32[]{:S(2)}) %all-to-all-start.2) | async-done | bytes 524320 | tf_op jit(solution)/shard_map/all_to_all | solution.py:169
  120.6 1.5 %place.1 = f32[64,8,512]{2,1,0:T(8,128)} custom-call(s32[3]{0:T(128)S(1)} %pad_add_fusion.coord_ref, bf16[32,16,512]{2,1,0:T(8,128)(2,1)S(1)} %all-to-all-done.2.every_ref), custom_call_target="tpu_custom_call" | custom-call | tf_op jit(solution)/shard_map/place/pallas_call | solution.py:252
  (5 shorter events, 0.0 us)
Async XLA Ops:
  3.5 41.3 %all-to-all-start = ((bf16[32,80,128]{2,1,0:T(8,128)(2,1)}), bf16[32,80,128]{2,1,0:T(8,128)(2,1)S(1)}, u32[]{:S(2)}, u32[]{:S(2)}) async-start(bf16[32,80,128]{2,1,0:T(8,128)(2,1)} %bitcast.21), calls=%async_computation | async-start | bytes 1310720 | tf_op jit(solution)/shard_map/all_to_all | solution.py:212
  22.0 22.8 %collective-permute-start = (bf16[2,8,512]{2,1,0:T(8,128)(2,1)S(1)}, bf16[2,8,512]{2,1,0:T(8,128)(2,1)S(1)}, u32[]{:S(2)}, u32[]{:S(2)}) collective-permute-start(bf16[2,8,512]{2,1,0:T(8,128)(2,1)S(1)} %get-tuple-element.8), channel_id=1, source_target_pairs={{0,16},{1,33},{2,18},{3,35},{4,20},{5,37},{6,22},{7,39},{8,24},{9,... | collective-permute-start | bytes 49160 | tf_op jit(solution)/shard_map/ppermute | solution.py:179
  41.5 3.2 %collective-permute-start.1 = (bf16[2,8,512]{2,1,0:T(8,128)(2,1)S(1)}, bf16[2,8,512]{2,1,0:T(8,128)(2,1)S(1)}, u32[]{:S(2)}, u32[]{:S(2)}) collective-permute-start(bf16[2,8,512]{2,1,0:T(8,128)(2,1)S(1)} %get-tuple-element.9), channel_id=1, source_target_pairs={{0,48},{1,1},{2,50},{3,3},{4,52},{5,5},{6,54},{7,7},{8,56},{9,9},{... | collective-permute-start | bytes 49160 | tf_op jit(solution)/shard_map/ppermute | solution.py:179
  45.9 63.1 %copy-start = (s32[1,2]{1,0:T(1,128)S(1)}, s32[1,2]{1,0:T(1,128)}, u32[]{:S(2)}) copy-start(s32[1,2]{1,0:T(1,128)} %param.7) | copy-start | bytes 28
  45.9 30.9 %all-to-all-start.1 = ((bf16[32,144,128]{2,1,0:T(8,128)(2,1)}), bf16[32,144,128]{2,1,0:T(8,128)(2,1)S(1)}, u32[]{:S(2)}, u32[]{:S(2)}) async-start(bf16[32,144,128]{2,1,0:T(8,128)(2,1)} %sum.1), calls=%async_computation.1 | async-start | bytes 2359296 | tf_op jit(solution)/shard_map/all_to_all | solution.py:229
  80.5 22.9 %collective-permute-start.2 = (bf16[2,8,512]{2,1,0:T(8,128)(2,1)S(1)}, bf16[2,8,512]{2,1,0:T(8,128)(2,1)S(1)}, u32[]{:S(2)}, u32[]{:S(2)}) collective-permute-start(bf16[2,8,512]{2,1,0:T(8,128)(2,1)S(1)} %get-tuple-element.10), channel_id=1, source_target_pairs={{0,16},{1,33},{2,18},{3,35},{4,20},{5,37},{6,22},{7,39},{8,24},{9,... | collective-permute-start | bytes 49160 | tf_op jit(solution)/shard_map/ppermute | solution.py:179
  93.1 10.2 %collective-permute-start.3 = (bf16[2,8,512]{2,1,0:T(8,128)(2,1)S(1)}, bf16[2,8,512]{2,1,0:T(8,128)(2,1)S(1)}, u32[]{:S(2)}, u32[]{:S(2)}) collective-permute-start(bf16[2,8,512]{2,1,0:T(8,128)(2,1)S(1)} %get-tuple-element.11), channel_id=1, source_target_pairs={{0,48},{1,1},{2,50},{3,3},{4,52},{5,5},{6,54},{7,7},{8,56},{9,9},{... | collective-permute-start | bytes 49160 | tf_op jit(solution)/shard_map/ppermute | solution.py:179
  104.2 16.4 %all-to-all-start.2 = ((bf16[32,16,512]{2,1,0:T(8,128)(2,1)}), bf16[32,16,512]{2,1,0:T(8,128)(2,1)S(1)}, u32[]{:S(2)}, u32[]{:S(2)}) async-start(bf16[32,16,512]{2,1,0:T(8,128)(2,1)} %fan.1), calls=%async_computation.2 | async-start | bytes 1048576 | tf_op jit(solution)/shard_map/all_to_all | solution.py:169
